TPU v7x, 32 devices: a whole 2x2x4 slice. The times are simulated.
32 devices in a mesh: ctx: 4 (over y, x), fsdp: 8 (over z, core).
Axes of the slice: x: 2, y: 2, z: 4, core: 2. Of those that a mesh axis runs over, the one named last changes fastest.
Arguments:
- tokens: bfloat16 [8192, 2048], P(('ctx', 'fsdp')), may hold values from -6 to 6
- routes: int32 [8192, 4], P(('ctx', 'fsdp')), may hold values from 0 to 7, all different within a row; in each aligned block of 256 rows (0 to 255, 256 to 511, ...) at most 176 rows name the same one
- block_ids: int32 [8], replicated, may hold values from 0 to 7, as said below
- attn_gain: bfloat16 [2048], P('fsdp'), may hold values from 0.099609375 to 1.8984375
- w_attn_in: bfloat16 [2048, 6144], P('fsdp'), may hold values from -0.125 to 0.125
- b_qkv: bfloat16 [6144], P('fsdp'), may hold values from -2 to 2
- w_attn_out: bfloat16 [2048, 2048], P('fsdp'), may hold values from -1 to 1
- ffn_gain: bfloat16 [2048], P('fsdp'), may hold values from 0.099609375 to 1.8984375
- router: bfloat16 [2048, 8], P('fsdp'), may hold values from -0.0625 to 0.0625
- shared_gate: bfloat16 [2048], P('fsdp'), may hold values from -0.125 to 0.125
- w_sh_in: bfloat16 [2048, 11264], P('fsdp'), may hold values from -0.125 to 0.125
- w_sh_out: bfloat16 [2048, 5632], P('fsdp'), may hold values from -0.21875 to 0.21875
- w_exp_in: bfloat16 [8, 2048, 2816], P(None, 'fsdp'), may hold values from -0.125 to 0.125
- w_exp_out: bfloat16 [8, 2048, 1408], P(None, 'fsdp'), may hold values from -0.625 to 0.625
- cotangent: bfloat16 [8192, 2048], P(('ctx', 'fsdp')), may hold values from -6 to 6
Outputs:
- block_out: bfloat16 [8192, 2048], P(('ctx', 'fsdp'))
- d_tokens: float32 [8192, 2048], P(('ctx', 'fsdp'))
- d_attn_gain: float32 [2048], P('fsdp')
- d_w_attn_in: float32 [2048, 6144], P('fsdp')
- d_b_qkv: float32 [6144], P('fsdp')
- d_w_attn_out: float32 [2048, 2048], P('fsdp')
- d_ffn_gain: float32 [2048], P('fsdp')
- d_router: float32 [2048, 8], P('fsdp')
- d_shared_gate: float32 [2048], P('fsdp')
- d_w_sh_in: float32 [2048, 11264], P('fsdp')
- d_w_sh_out: float32 [2048, 5632], P('fsdp')
- d_w_exp_in: float32 [8, 2048, 2816], P(None, 'fsdp')
- d_w_exp_out: float32 [8, 2048, 1408], P(None, 'fsdp')
Inputs may be any that keep to these rules, and one draw needn't show every extreme that they name: `routes`: each row names 4 different experts. Within the rows of one device no expert is named by more than 176 rows, and in every draw some expert is named by exactly 176 rows of some device. `block_ids`: entries 2c and 2c + 1 are the blocks of positions, of 128 tokens each, whose rows ctx index c holds, in that order; the two numbers add up to 7, and every number appears once.
All inputs are finite; a program needn't handle non-finite values.
Results may differ from a plain program's by a relative error of at most 0.035.
Values may be sent and summed in bfloat16 or wider, within the bound.
No kernel may reach another device: no remote copies, remote signals or barrier semaphores. Data moves between devices by JAX's collectives and lax.ppermute only.
A program may use at most 704 MiB of HBM per device.

v0:
```python
import functools

import jax
import jax.numpy as jnp
from jax import lax
from jax.experimental import pallas as pl
from jax.experimental.pallas import tpu as pltpu
from jax.sharding import PartitionSpec as P

D = 2048
HEADS = 16
HEAD_DIM = 128
FS = 5632
FE = 1408
EXPERTS = 8


norm_eps = 1e-06
rope_base = 1000000.0
highest = lax.Precision.HIGHEST


def rms_scale(values):
    return lax.rsqrt(jnp.mean(values * values, axis=1, keepdims=True) + norm_eps)


def rms_back(grad_rows, unit_rows, row_scale, gain_row):
    scaled = grad_rows * gain_row
    return row_scale * (scaled - unit_rows * jnp.mean(scaled * unit_rows, axis=1, keepdims=True))


def block_places(block_list, block_len):
    offsets = jnp.arange(block_len, dtype=jnp.int32)
    return (block_list[:, None] * block_len + offsets[None, :]).reshape(-1)


def rotary_tables(positions):
    half_dim = HEAD_DIM // 2
    inverse = rope_base ** (-2.0 * jnp.arange(half_dim, dtype=jnp.float32) / HEAD_DIM)
    angles = positions.astype(jnp.float32)[:, None] * inverse[None, :]
    cos_table = jnp.cos(angles)
    sin_table = jnp.sin(angles)
    return (
        jnp.concatenate([cos_table, cos_table], axis=1),
        jnp.concatenate([sin_table, sin_table], axis=1),
    )


def rotate(values, cos_table, sin_table):
    half_dim = HEAD_DIM // 2
    turned = jnp.concatenate([-values[..., half_dim:], values[..., :half_dim]], axis=-1)
    return values * cos_table[:, None, :] + turned * sin_table[:, None, :]


def unrotate(values, cos_table, sin_table):
    half_dim = HEAD_DIM // 2
    scaled = values * sin_table[:, None, :]
    turned = jnp.concatenate([scaled[..., half_dim:], -scaled[..., :half_dim]], axis=-1)
    return values * cos_table[:, None, :] + turned


def swiglu(activation, breadth):
    return jax.nn.silu(activation[:, :breadth]) * activation[:, breadth:]


def swiglu_back(grad_hidden, activation, breadth):
    gate_part = activation[:, :breadth]
    up_part = activation[:, breadth:]
    sig_gate = jax.nn.sigmoid(gate_part)
    d_gate = grad_hidden * up_part * sig_gate * (1.0 + gate_part * (1.0 - sig_gate))
    d_up = grad_hidden * gate_part * sig_gate
    return jnp.concatenate([d_gate, d_up], axis=1)


def outer_rows(left_ops, right_ops):
    pieces = []
    for left_op, right_op in zip(left_ops, right_ops):
        pieces.append(
            lax.dot_general(
                left_op, right_op, (((0,), (0,)), ((), ())), preferred_element_type=jnp.float32
            )
        )
    return jnp.concatenate(pieces, axis=1)


def right_product(left_op, right_op):
    return lax.dot_general(
        left_op, right_op, (((1,), (1,)), ((), ())), preferred_element_type=jnp.float32
    )


def to_peer(array, bits):
    size = lax.axis_size("ctx")
    return lax.ppermute(array, "ctx", [(rank, rank ^ bits) for rank in range(size)])


def peer_gather(array, direct=False):
    size = lax.axis_size("ctx")
    if size != 4 or direct:
        return [array] + [to_peer(array, bits) for bits in range(1, size)]
    half = array.shape[0] // 2
    one, two = to_peer(array, 1), to_peer(array, 2)
    three = jnp.concatenate([to_peer(one[:half], 2), to_peer(two[half:], 1)], axis=0)
    return [array, one, two, three]


def wide(array):
    return array.astype(jnp.float32)


def low(array):
    return array.astype(jnp.bfloat16)


def peer_scatter(pieces):
    size = lax.axis_size("ctx")
    pieces = [low(piece) for piece in pieces]
    if size != 4:
        total = wide(pieces[0])
        for bits in range(1, size):
            total = total + wide(to_peer(pieces[bits], bits))
        return total
    half = pieces[0].shape[0] // 2
    first = to_peer(jnp.concatenate([pieces[1][:half], pieces[3][:half]], axis=0), 1)
    second = to_peer(jnp.concatenate([pieces[2][half:], pieces[3][half:]], axis=0), 2)
    upper = to_peer(low(wide(pieces[2][:half]) + wide(first[half:])), 2)
    lower = to_peer(low(wide(pieces[1][half:]) + wide(second[half:])), 1)
    return wide(pieces[0]) + jnp.concatenate(
        [wide(first[:half]) + wide(upper), wide(second[:half]) + wide(lower)], axis=0
    )


def peer_sum(array):
    size, half = lax.axis_size("ctx"), array.shape[0] // 2
    upper, lower, bits = array[:half], array[half:], 1
    while bits < size:
        upper, lower = low(upper), low(lower)
        other = size // 2 // bits
        upper = wide(upper) + wide(to_peer(upper, bits))
        lower = wide(lower) + wide(to_peer(lower, other))
        bits *= 2
    return jnp.concatenate([upper, lower], axis=0)


def by_rank(pieces):
    rank, bits = lax.axis_index("ctx"), 1
    while bits < len(pieces):
        odd = (rank & bits) != 0
        pieces = [jnp.where(odd, pieces[k ^ bits], pieces[k]) for k in range(len(pieces))]
        bits *= 2
    return pieces


def to_mate(array, bits):
    size = lax.axis_size("fsdp")
    return lax.ppermute(array, "fsdp", [(rank, rank ^ bits) for rank in range(size)])


def total_sum(array):
    bits = 1
    while bits < lax.axis_size("fsdp"):
        array = array + to_mate(array, bits)
        bits *= 2
    bits = 1
    while bits < lax.axis_size("ctx"):
        array = array + to_peer(array, bits)
        bits *= 2
    return array


VMEM_BYTES = 56 * 1024 * 1024


def own_call(kernel, name, grid, ins, in_specs, outs, out_specs, flops, waits=(), order=None, aliases=None):
    lead = 0 if order is None else 1
    count = len(ins)

    def body(*refs):
        kernel(*refs[lead : lead + count], *refs[lead + count + len(waits) :])

    moved = sum(array.size * array.dtype.itemsize for array in [*ins, *outs])
    return pl.pallas_call(
        body,
        out_shape=list(outs),
        grid_spec=pltpu.PrefetchScalarGridSpec(
            num_scalar_prefetch=lead,
            grid=grid,
            in_specs=list(in_specs) + [pl.BlockSpec(memory_space=pl.ANY)] * len(waits),
            out_specs=list(out_specs),
        ),
        compiler_params=pltpu.CompilerParams(vmem_limit_bytes=VMEM_BYTES),
        cost_estimate=pl.CostEstimate(flops=flops, transcendentals=0, bytes_accessed=moved),
        input_output_aliases=aliases or {},
        name=name,
    )(*([] if order is None else [order]), *ins, *waits)


def after(array, waits):
    waits = [wait for wait in waits if wait is not None]
    if not waits:
        return array
    return pl.pallas_call(
        lambda *refs: None,
        out_shape=jax.ShapeDtypeStruct(array.shape, array.dtype),
        in_specs=[pl.BlockSpec(memory_space=pl.ANY)] * (1 + len(waits)),
        out_specs=pl.BlockSpec(memory_space=pl.ANY),
        input_output_aliases={0: 0},
        name="after",
    )(array, *waits)


def unit_backward(rows_in, rows_grad, weight, factor, waits=()):
    rows, depth = rows_in.shape
    breadth = weight.shape[1] // 3
    if breadth % 128:
        act = jnp.dot(rows_in, weight[:, : 2 * breadth], preferred_element_type=jnp.float32)
        d_unit = jnp.dot(rows_grad, weight[:, 2 * breadth :], preferred_element_type=jnp.float32)
        units = swiglu(act, breadth)
        return (
            low(factor * units),
            low(swiglu_back(factor * d_unit, act, breadth)),
            jnp.sum(d_unit * units, axis=1, keepdims=True),
        )
    tall = min(rows, 256)

    def kernel(rows_ref, grad_ref, weight_ref, factor_ref, out_ref, d_act_ref, d_factor_ref):
        scale = factor_ref[...]
        total = jnp.zeros((tall, 1), jnp.float32)
        for start in range(0, breadth, 256):
            gate = slice(start, min(start + 256, breadth))
            up = slice(breadth + gate.start, breadth + gate.stop)
            down = slice(2 * breadth + gate.start, 2 * breadth + gate.stop)
            gate_part = jnp.dot(
                rows_ref[...], weight_ref[:, gate], preferred_element_type=jnp.float32
            )
            up_part = jnp.dot(rows_ref[...], weight_ref[:, up], preferred_element_type=jnp.float32)
            d_unit = jnp.dot(grad_ref[...], weight_ref[:, down], preferred_element_type=jnp.float32)
            sig_gate = jax.nn.sigmoid(gate_part)
            silu = gate_part * sig_gate
            units = silu * up_part
            total = total + jnp.sum(d_unit * units, axis=1, keepdims=True)
            out_ref[:, gate] = low(scale * units)
            scaled = scale * d_unit
            d_act_ref[:, gate] = low(scaled * up_part * (sig_gate + silu * (1.0 - sig_gate)))
            d_act_ref[:, up] = low(scaled * silu)
        d_factor_ref[...] = total

    return own_call(
        kernel,
        "unit_backward",
        (rows // tall,),
        [rows_in, rows_grad, weight, factor],
        [
            pl.BlockSpec((tall, depth), lambda i: (i, 0)),
            pl.BlockSpec((tall, depth), lambda i: (i, 0)),
            pl.BlockSpec((depth, 3 * breadth), lambda i: (0, 0)),
            pl.BlockSpec((tall, 1), lambda i: (i, 0)),
        ],
        [
            jax.ShapeDtypeStruct((rows, breadth), jnp.bfloat16),
            jax.ShapeDtypeStruct((rows, 2 * breadth), jnp.bfloat16),
            jax.ShapeDtypeStruct((rows, 1), jnp.float32),
        ],
        [
            pl.BlockSpec((tall, breadth), lambda i: (i, 0)),
            pl.BlockSpec((tall, 2 * breadth), lambda i: (i, 0)),
            pl.BlockSpec((tall, 1), lambda i: (i, 0)),
        ],
        6 * rows * depth * breadth,
        waits,
    )


def back_matmul(jobs, waits=()):
    rows, breadth = jobs[0][0][0][0].shape[0], jobs[0][0][0][1].shape[0]
    tile = 256
    ins, specs, flops = [], [], 0
    for products, total, dtype in jobs:
        for rows_in, weight, column in products:
            depth = rows_in.shape[1]
            if depth % 128 and weight.shape[1] != depth:
                weight = weight[:, column * depth : (column + 1) * depth]
                column = 0
            ins += [rows_in, weight]
            specs += [
                pl.BlockSpec((rows, depth), lambda j: (0, 0)),
                pl.BlockSpec((tile, depth), lambda j, column=column: (j, column)),
            ]
            flops += 2 * rows * depth * breadth
        if total is not None:
            ins.append(total)
            specs.append(pl.BlockSpec((rows, tile), lambda j: (0, j)))

    def kernel(*refs):
        used = 0
        for out, (products, total, dtype) in enumerate(jobs):
            value = None
            for _ in products:
                part = right_product(refs[used][...], refs[used + 1][...])
                value = part if value is None else value + part
                used += 2
            if total is not None:
                value = value + wide(refs[used][...])
                used += 1
            refs[len(ins) + out][...] = value.astype(dtype)

    return own_call(
        kernel,
        "back_matmul",
        (breadth // tile,),
        ins,
        specs,
        [jax.ShapeDtypeStruct((rows, breadth), dtype) for products, total, dtype in jobs],
        [pl.BlockSpec((rows, tile), lambda j: (0, j))] * len(jobs),
        flops,
        waits,
    )


def route_product(d_route, route_mat):
    coarse = low(d_route)
    fine = low(d_route - wide(coarse))
    both = low(jnp.concatenate([route_mat, route_mat], axis=1))
    return (jnp.concatenate([coarse, fine], axis=1), both, 0)


def grad_matmul(pairs, waits=()):
    blocks = lax.axis_size("fsdp")
    depth = pairs[0][0][0].shape[1]
    widths = [rights[0].shape[1] for lefts, rights in pairs]
    total, block = sum(widths), depth // blocks
    ins, specs, flops = [], [], 0
    for lefts, rights in pairs:
        for left, right in zip(lefts, rights):
            ins += [left, right]
            specs += [
                pl.BlockSpec((left.shape[0], block), lambda j: (0, j)),
                pl.BlockSpec(right.shape, lambda j: (0, 0)),
            ]
            flops += 2 * left.shape[0] * depth * right.shape[1]

    def kernel(*refs):
        start, used = 0, 0
        for (lefts, rights), width in zip(pairs, widths):
            value = None
            for _ in lefts:
                part = lax.dot_general(
                    refs[used][...],
                    refs[used + 1][...],
                    (((0,), (0,)), ((), ())),
                    preferred_element_type=jnp.float32,
                )
                value = part if value is None else value + part
                used += 2
            refs[-1][:, start : start + width] = low(value)
            start += width

    return own_call(
        kernel,
        "grad_matmul",
        (blocks,),
        ins,
        specs,
        [jax.ShapeDtypeStruct((depth, total), jnp.bfloat16)],
        [pl.BlockSpec((block, total), lambda j: (j, 0))],
        flops,
        waits,
    )[0]


def split_matmul(rows_in, gain, weight, bias, cos_table, sin_table, waits=()):
    rows, depth = rows_in.shape
    breadth = bias.shape[0]
    tile = 256
    turned = breadth * 2 // 3 // tile
    tall = min(rows, 256)

    def kernel(rows_ref, gain_ref, weight_ref, bias_ref, cos_ref, sin_ref, normed_ref, out_ref):
        @pl.when(pl.program_id(0) == 0)
        def _():
            for start in range(0, rows, tall):
                some = slice(start, start + tall)
                values = wide(rows_ref[some, :])
                normed_ref[some, :] = low(values * rms_scale(values) * gain_ref[...])

        value = jnp.dot(normed_ref[...], weight_ref[...], preferred_element_type=jnp.float32)
        value = value + bias_ref[...]

        @pl.when(pl.program_id(0) < turned)
        def _():
            for start in range(0, tile, HEAD_DIM):
                head = value[:, start : start + HEAD_DIM]
                head = head * cos_ref[...] + pltpu.roll(head, HEAD_DIM // 2, 1) * sin_ref[...]
                out_ref[:, start : start + HEAD_DIM] = low(head)

        @pl.when(pl.program_id(0) >= turned)
        def _():
            out_ref[...] = low(value)

    whole = pl.BlockSpec((rows, depth), lambda j: (0, 0))
    table = pl.BlockSpec((rows, HEAD_DIM), lambda j: (0, 0))
    return own_call(
        kernel,
        "split_matmul",
        (breadth // tile,),
        [rows_in, gain.reshape(1, depth), weight, bias.reshape(1, breadth), cos_table, sin_table],
        [
            whole,
            pl.BlockSpec((1, depth), lambda j: (0, 0)),
            pl.BlockSpec((depth, tile), lambda j: (0, j)),
            pl.BlockSpec((1, tile), lambda j: (0, j)),
            table,
            table,
        ],
        [
            jax.ShapeDtypeStruct((rows, depth), jnp.bfloat16),
            jax.ShapeDtypeStruct((rows, breadth), jnp.bfloat16),
        ],
        [whole, pl.BlockSpec((rows, tile), lambda j: (0, j))],
        2 * rows * depth * breadth,
        waits,
    )


def head_specs(rows, heads):
    return [
        pl.BlockSpec((rows, HEAD_DIM), lambda h, part=part: (0, part * heads + h))
        for part in range(3)
    ]


def attend(split, places, heads, waits=()):
    rows = split.shape[0]
    tall = min(rows, 256)
    scale = HEAD_DIM ** (-0.5)

    def kernel(query_ref, key_ref, value_ref, down_ref, across_ref, out_ref, log_ref):
        for start in range(0, rows, tall):
            some = slice(start, start + tall)
            scores = right_product(query_ref[some, :], key_ref[...]) * scale
            scores = jnp.where(across_ref[...] <= down_ref[some, :], scores, -1e30)
            top = jnp.max(scores, axis=1, keepdims=True)
            exponent = jnp.exp(scores - top)
            total = jnp.sum(exponent, axis=1, keepdims=True)
            prob = low(exponent * (1.0 / total))
            out_ref[some, :] = low(
                jnp.dot(prob, value_ref[...], preferred_element_type=jnp.float32)
            )
            log_ref[some, :] = top + jnp.log(total)

    return own_call(
        kernel,
        "attend",
        (heads,),
        [split, split, split, places.reshape(rows, 1), places.reshape(1, rows)],
        head_specs(rows, heads)
        + [
            pl.BlockSpec((rows, 1), lambda h: (0, 0)),
            pl.BlockSpec((1, rows), lambda h: (0, 0)),
        ],
        [
            jax.ShapeDtypeStruct((rows, heads * HEAD_DIM), jnp.bfloat16),
            jax.ShapeDtypeStruct((heads, rows, 1), jnp.float32),
        ],
        [
            pl.BlockSpec((rows, HEAD_DIM), lambda h: (0, h)),
            pl.BlockSpec((None, rows, 1), lambda h: (h, 0, 0)),
        ],
        4 * rows * rows * heads * HEAD_DIM,
        waits,
    )


def attend_back(split, places, log_total, d_vec, cos_table, sin_table, heads, waits=()):
    rows = split.shape[0]
    tall = min(rows, 256)
    scale = HEAD_DIM ** (-0.5)

    def kernel(query_ref, key_ref, value_ref, down_ref, across_ref, log_ref, grad_ref, cos_ref, sin_ref, out_ref):
        first = pl.multiple_of(pl.program_id(0) * HEAD_DIM, HEAD_DIM)
        d_key = jnp.zeros((rows, HEAD_DIM), jnp.float32)
        d_value = jnp.zeros((rows, HEAD_DIM), jnp.float32)

        def unturned(grad, some):
            return low(
                grad * cos_ref[some, :]
                - pltpu.roll(grad, HEAD_DIM // 2, 1) * sin_ref[some, :]
            )

        def columns(part):
            return pl.ds(first + part * heads * HEAD_DIM, HEAD_DIM)

        for start in range(0, rows, tall):
            some = slice(start, start + tall)
            query, grad = query_ref[some, :], grad_ref[some, :]
            scores = right_product(query, key_ref[...]) * scale
            prob = jnp.where(
                across_ref[...] <= down_ref[some, :], jnp.exp(scores - log_ref[some, :]), 0.0
            )
            d_prob = right_product(grad, value_ref[...])
            inner = jnp.sum(prob * d_prob, axis=1, keepdims=True)
            d_score = low(prob * (d_prob - inner) * scale)
            across = (((0,), (0,)), ((), ()))
            d_value = d_value + lax.dot_general(
                low(prob), grad, across, preferred_element_type=jnp.float32
            )
            d_key = d_key + lax.dot_general(
                d_score, query, across, preferred_element_type=jnp.float32
            )
            d_query = jnp.dot(d_score, key_ref[...], preferred_element_type=jnp.float32)
            out_ref[some, columns(0)] = unturned(d_query, some)
        out_ref[:, columns(1)] = unturned(d_key, slice(0, rows))
        out_ref[:, columns(2)] = low(d_value)

    table = pl.BlockSpec((rows, HEAD_DIM), lambda h: (0, 0))
    return own_call(
        kernel,
        "attend_back",
        (heads,),
        [split, split, split, places.reshape(rows, 1), places.reshape(1, rows), log_total, d_vec]
        + [cos_table, sin_table],
        head_specs(rows, heads)
        + [
            pl.BlockSpec((rows, 1), lambda h: (0, 0)),
            pl.BlockSpec((1, rows), lambda h: (0, 0)),
            pl.BlockSpec((None, rows, 1), lambda h: (h, 0, 0)),
            pl.BlockSpec((rows, HEAD_DIM), lambda h: (0, h)),
            table,
            table,
        ],
        [jax.ShapeDtypeStruct((rows, 3 * heads * HEAD_DIM), jnp.bfloat16)],
        [pl.BlockSpec((rows, 3 * heads * HEAD_DIM), lambda h: (0, 0))],
        10 * rows * rows * heads * HEAD_DIM,
        waits,
    )[0]


def place_grads(spread, slot, slots, totals, waits=()):
    size, rows = len(spread[0][0]), spread[0][0][0].shape[0]
    units = sum([sum(parts) for pieces, parts in spread])
    if units % 128:
        ordered = by_rank(spread[0][0])
        sides = [
            jnp.stack([piece[:, k * units : (k + 1) * units] for piece in ordered], axis=1)
            for k in range(3)
        ]
        into = jnp.stack(sides[:2], axis=1).reshape(rows, 2 * size * units)
        return wide(into), wide(sides[2].reshape(rows, size * units))
    tall = min(rows, 64)
    columns = 2 if slot is None else 1
    pieces = [held[k] for k in range(size) for held, parts in spread]
    onto = [] if totals is None else list(totals)
    rest = list(waits) + onto
    steps = rows // tall

    def kernel(*refs):
        in_ref, out_ref = refs[-2:]
        for k in range(size):

            @pl.when(pl.program_id(0) == k)
            def _():
                used = refs[k * len(spread) : (k + 1) * len(spread)]
                place = 0
                for (held, parts), ref in zip(spread, used):
                    start = 0
                    for part in parts:
                        gate = ref[:, start : start + part]
                        up = ref[:, start + part : start + 2 * part]
                        if slot is None:
                            here = pl.program_id(2) == 0
                            in_ref[:, place : place + part] = wide(jnp.where(here, gate, up))
                        else:
                            in_ref[:, place : place + part] = wide(gate)
                            in_ref[:, units + place : units + place + part] = wide(up)
                        out_ref[:, place : place + part] = wide(
                            ref[:, start + 2 * part : start + 3 * part]
                        )
                        place += part
                        start += 3 * part

    def piece_spec(k, parts):
        def piece_map(step, row, column, rank_ref):
            return (jnp.where(step == k, row, jnp.where(step < k, 0, steps - 1)), 0)

        return pl.BlockSpec((tall, 3 * sum(parts)), piece_map)

    if slot is None:
        shapes = [(rows, 2 * size * units), (rows, size * units)]
        out_specs = [
            pl.BlockSpec(
                (tall, units),
                lambda k, row, column, rank_ref: (row, column * size + (rank_ref[0] ^ k)),
            ),
            pl.BlockSpec((tall, units), lambda k, row, column, rank_ref: (row, rank_ref[0] ^ k)),
        ]
    else:
        shapes = [(size * slots, rows, 2 * units), (size * slots, rows, units)]
        out_specs = [
            pl.BlockSpec(
                (None, tall, shape[2]),
                lambda k, row, column, rank_ref: ((rank_ref[0] ^ k) * slots + slot, row, 0),
            )
            for shape in shapes
        ]
    first = 1 + len(pieces) + len(waits)
    return own_call(
        kernel,
        "place_grads",
        (size, steps, columns),
        pieces,
        [piece_spec(k, parts) for k in range(size) for held, parts in spread],
        [jax.ShapeDtypeStruct(shape, jnp.float32) for shape in shapes],
        out_specs,
        0,
        rest,
        lax.axis_index("ctx").reshape(1),
        aliases={first: 0, first + 1: 1} if onto else {},
    )


def place_cols(pieces, parts, waits=()):
    size, rows = len(pieces), pieces[0].shape[0]
    breadth = pieces[0].shape[1] // parts
    if breadth % 128:
        ordered = [piece.reshape(rows, parts, breadth) for piece in by_rank(pieces)]
        return wide(jnp.stack(ordered, axis=2).reshape(rows, parts * size * breadth))

    def kernel(*refs):
        for k, ref in enumerate(refs[:-1]):

            @pl.when(pl.program_id(0) == k)
            def _():
                refs[-1][...] = wide(ref[...])

    def piece_spec(own):
        def piece_map(k, part, rank_ref):
            return (0, jnp.where(k == own, part, jnp.where(k < own, 0, parts - 1)))

        return pl.BlockSpec((rows, breadth), piece_map)

    return own_call(
        kernel,
        "place_cols",
        (size, parts),
        pieces,
        [piece_spec(own) for own in range(size)],
        [jax.ShapeDtypeStruct((rows, parts * size * breadth), jnp.float32)],
        [
            pl.BlockSpec(
                (rows, breadth), lambda k, part, rank_ref: (0, part * size + (rank_ref[0] ^ k))
            )
        ],
        0,
        waits,
        lax.axis_index("ctx").reshape(1),
    )[0]

def per_device(
    tokens,
    routes,
    block_ids,
    attn_gain,
    w_attn_in,
    b_qkv,
    w_attn_out,
    ffn_gain,
    router,
    shared_gate,
    w_sh_in,
    w_sh_out,
    w_exp_in,
    w_exp_out,
    cotangent,
):
    ctx_size = lax.axis_size("ctx")
    fsdp_size = lax.axis_size("fsdp")
    ctx_rank = lax.axis_index("ctx")
    fsdp_rank = lax.axis_index("fsdp")
    tok_rows = tokens.shape[0]
    block_len = tok_rows // 2
    seq_len = tok_rows * ctx_size
    heads_own = HEADS // ctx_size
    att_cols = heads_own * HEAD_DIM
    sh_cols = FS // ctx_size
    experts_own = EXPERTS // ctx_size

    def own_cols(array, start, breadth):
        return lax.dynamic_slice_in_dim(array, start + ctx_rank * breadth, breadth, axis=1)

    def gather_fsdp(array):
        return lax.all_gather(array, "fsdp", axis=0, tiled=True)

    def scatter_fsdp(array):
        return lax.psum_scatter(
            array.astype(jnp.bfloat16), "fsdp", scatter_dimension=0, tiled=True
        )

    def token_pieces(array):
        return [array[k * tok_rows : (k + 1) * tok_rows] for k in range(ctx_size)]

    tokens_all = jnp.concatenate(peer_gather(tokens), axis=0)
    quarter = D // ctx_size
    w_out_own = gather_fsdp(own_cols(w_attn_out, 0, quarter))
    w_out_pieces = peer_gather(w_out_own)
    rows = attn_gain.shape[0]
    smalls = jnp.concatenate(
        [jnp.stack([attn_gain, ffn_gain, shared_gate], axis=1), router, b_qkv.reshape(3, rows).T],
        axis=1,
    )
    smalls = jnp.pad(smalls, ((0, 0), (0, 128 - smalls.shape[1])))
    w_in_slab = jnp.concatenate(
        [own_cols(w_attn_in, part * D, att_cols) for part in range(3)] + [smalls], axis=1
    )
    w_in_own = gather_fsdp(after(w_in_slab, [w_out_own]))
    smalls_all = w_in_own[:, 3 * att_cols :]
    gain_one, gain_two, gate_vec = [wide(smalls_all[:, k]) for k in range(3)]
    router_wide = wide(smalls_all[:, 3 : 3 + EXPERTS])
    bias_full = smalls_all[:, 3 + EXPERTS : 6 + EXPERTS].reshape(fsdp_size, rows, 3)
    bias_full = jnp.transpose(bias_full, (0, 2, 1)).reshape(3, D)
    bias_own = wide(own_cols(bias_full, 0, att_cols)).reshape(3 * att_cols)

    slabs = [
        [own_cols(w_sh_in, part * FS, sh_cols) for part in range(2)]
        + [own_cols(w_sh_out, 0, sh_cols)]
    ]
    for own in range(experts_own):
        expert = ctx_rank * experts_own + own
        slabs.append([w_exp_in[expert, :, :FE], w_exp_in[expert, :, FE:], w_exp_out[expert]])
    slabs = [jnp.concatenate(sides, axis=1) for sides in slabs]

    inputs = wide(tokens)
    scale_one = rms_scale(inputs)
    unit_one = inputs * scale_one
    ranks = ctx_rank ^ jnp.arange(ctx_size, dtype=jnp.int32)
    places = block_places(block_ids.reshape(ctx_size, 2)[ranks].reshape(-1), block_len)
    cos_table, sin_table = rotary_tables(places)
    half = HEAD_DIM // 2
    sin_table = jnp.concatenate([-sin_table[:, :half], sin_table[:, half:]], axis=1)
    normed_all, split = split_matmul(
        tokens_all, gain_one, w_in_own, bias_own, cos_table, sin_table
    )
    attended, log_total = attend(split, places, heads_own, w_out_pieces)
    head_pieces = token_pieces(attended)
    head_pieces = head_pieces[:1] + [
        to_peer(head_pieces[bits], bits) for bits in range(1, ctx_size)
    ]
    attn_vec = jnp.concatenate(by_rank(head_pieces), axis=1)
    attn_out = [
        jnp.dot(attn_vec, piece, preferred_element_type=jnp.float32) for piece in w_out_pieces
    ]
    residual = inputs + jnp.concatenate(by_rank(attn_out), axis=1)

    scale_two = rms_scale(residual)
    unit_two = residual * scale_two
    cots = [jnp.concatenate(peer_gather(after(cotangent, [split])), axis=0)]
    hidden_in = low(unit_two * gain_two)
    hidden = [jnp.concatenate(peer_gather(hidden_in), axis=0)]
    route_mat = jnp.concatenate([router_wide, gate_vec[:, None]], axis=1)
    expert_ids = jnp.arange(EXPERTS, dtype=jnp.int32)
    logits = jnp.dot(
        wide(hidden[0]), route_mat, precision=highest, preferred_element_type=jnp.float32
    )
    route_probs = jax.nn.softmax(logits[:, :EXPERTS], axis=1)
    shared_prob = jax.nn.sigmoid(logits[:, EXPERTS:])
    routes_all = jnp.concatenate(
        [routes] + [to_peer(routes, bits) for bits in range(1, ctx_size)], axis=0
    )
    chosen = wide(jnp.any(routes_all[:, :, None] == expert_ids[None, None, :], axis=1))

    weights = [
        gather_fsdp(after(slab, [wait]))
        for slab, wait in zip(slabs, (w_in_own, split, attended))
    ]
    d_probs = jnp.zeros((seq_len, EXPERTS), jnp.float32)
    sums, waits, grads = [None, None], [], []
    for index, weight in enumerate(weights):
        own = index - 1
        if own < 0:
            factor = shared_prob
        else:
            picked = (expert_ids == ctx_rank * experts_own + own)[None, :]
            factor = jnp.sum(
                jnp.where(picked, route_probs * chosen, 0.0), axis=1, keepdims=True
            )
        scaled_out, d_act, d_factor = unit_backward(hidden[0], cots[0], weight, factor, waits)
        if own < 0:
            d_gate_logit = d_factor * (shared_prob * (1.0 - shared_prob))
        else:
            d_probs = d_probs + jnp.where(picked, chosen * d_factor, 0.0)
        waits = [scaled_out]
        products, outward = [(d_act, weight, 0)], [(scaled_out, weight, 2)]
        if index == len(weights) - 1:
            d_logits = route_probs * (
                d_probs - jnp.sum(route_probs * d_probs, axis=1, keepdims=True)
            )
            d_route = jnp.concatenate([d_logits, d_gate_logit], axis=1)
            products.append(route_product(d_route, route_mat))
            d_hidden_sum = back_matmul([(products, sums[0], jnp.bfloat16)], waits)[0]
            waits = [d_hidden_sum]
        grads.append(grad_matmul([(hidden, [d_act]), (cots, [scaled_out])], waits))
        waits = [grads[-1]]
        if index < len(weights) - 1:
            sums = back_matmul(
                [(products, sums[0], jnp.float32), (outward, sums[1], jnp.float32)], waits
            )
            waits = [sums[0]]
    block_sum = back_matmul([(outward, sums[1], jnp.bfloat16)], waits)[0]
    waits = [block_sum]
    shards = [scatter_fsdp(grad) for grad in grads]
    d_route_mat = lax.dot_general(
        d_route,
        wide(hidden[0]),
        (((0,), (0,)), ((), ())),
        precision=highest,
        preferred_element_type=jnp.float32,
    )
    d_hidden = peer_scatter(token_pieces(d_hidden_sum))
    cot_wide = wide(cotangent)
    d_gain_two = jnp.sum(d_hidden * unit_two, axis=0)
    d_resid = cot_wide + rms_back(d_hidden, unit_two, scale_two, gain_two)
    d_attn = low(d_resid)
    d_attn_pieces = by_rank(
        [d_attn[:, k * quarter : (k + 1) * quarter] for k in range(ctx_size)]
    )
    products = [(piece, weight, 0) for piece, weight in zip(d_attn_pieces, w_out_pieces)]
    d_vec_own = back_matmul([(products, None, jnp.bfloat16)], waits)[0]
    d_vec_pieces = by_rank(
        [d_vec_own[:, k * att_cols : (k + 1) * att_cols] for k in range(ctx_size)]
    )
    d_vec = jnp.concatenate(
        d_vec_pieces[:1] + [to_peer(d_vec_pieces[bits], bits) for bits in range(1, ctx_size)],
        axis=0,
    )
    grad_w_out = grad_matmul(
        [([attn_vec], [jnp.concatenate(d_attn_pieces, axis=1)])], [d_vec_own]
    )
    grad_w_out = peer_scatter(
        [grad_w_out[:, k * quarter : (k + 1) * quarter] for k in range(ctx_size)]
    )
    grad_w_out = scatter_fsdp(grad_w_out)
    d_mixed = attend_back(split, places, log_total, d_vec, cos_table, sin_table, heads_own)
    grad_w_in = grad_matmul([([normed_all], [d_mixed])])
    d_bias = jnp.sum(wide(d_mixed), axis=0)
    d_normed_part = back_matmul(
        [([(d_mixed, w_in_own, 0)], None, jnp.bfloat16)], [grad_w_in]
    )[0]
    grad_w_in = scatter_fsdp(grad_w_in)
    d_normed = peer_scatter(token_pieces(d_normed_part))
    block_out = low(residual + peer_scatter(token_pieces(after(block_sum, [d_mixed]))))
    units, totals, waits = [sh_cols] + [FE] * experts_own, None, [d_normed_part]
    for own, shard in zip(range(-1, experts_own), shards):
        spread = [(peer_gather(after(shard, waits)), units[:1] if own < 0 else units[1:2])]
        if own < 0:
            shared_totals = place_grads(spread, None, 1, None, waits)
            waits = [shared_totals[0]]
        else:
            totals = place_grads(spread, own, experts_own, totals, waits)
    wide_all = wide(tokens_all)
    d_gain_one = jnp.sum(wide(d_normed_part) * (wide_all * rms_scale(wide_all)), axis=0)
    d_tokens = d_resid + rms_back(d_normed, unit_one, scale_one, gain_one)

    bias_spread = lax.dynamic_update_slice(
        jnp.zeros((3, D), jnp.float32), d_bias.reshape(3, att_cols), (0, ctx_rank * att_cols)
    )
    early_grads = total_sum(jnp.concatenate([d_route_mat.reshape(-1), d_gain_two]))
    late_grads = total_sum(jnp.concatenate([bias_spread.reshape(-1), d_gain_one]))

    def own_part(vector):
        size = vector.shape[0] // fsdp_size
        return lax.dynamic_slice_in_dim(vector, fsdp_rank * size, size)

    route_total = early_grads[: (EXPERTS + 1) * D].reshape(EXPERTS + 1, D)
    route_part = lax.dynamic_slice_in_dim(route_total, fsdp_rank * rows, rows, axis=1)
    return (
        block_out,
        d_tokens,
        own_part(late_grads[3 * D :]),
        place_cols(peer_gather(grad_w_in), 3, [totals[1]]),
        own_part(late_grads[: 3 * D]),
        wide(jnp.concatenate(by_rank(peer_gather(after(grad_w_out, totals[:1]))), axis=1)),
        own_part(early_grads[(EXPERTS + 1) * D :]),
        route_part[:EXPERTS].T,
        route_part[EXPERTS],
        *shared_totals,
        *totals,
    )


def solution(mesh):
    return jax.shard_map(
        per_device,
        mesh=mesh,
        in_specs=(
            P(("ctx", "fsdp"), None),
            P(("ctx", "fsdp"), None),
            P(),
            P("fsdp"),
            P("fsdp", None),
            P("fsdp"),
            P("fsdp", None),
            P("fsdp"),
            P("fsdp", None),
            P("fsdp"),
            P("fsdp", None),
            P("fsdp", None),
            P(None, "fsdp", None),
            P(None, "fsdp", None),
            P(("ctx", "fsdp"), None),
        ),
        out_specs=(
            P(("ctx", "fsdp"), None),
            P(("ctx", "fsdp"), None),
            P("fsdp"),
            P("fsdp", None),
            P("fsdp"),
            P("fsdp", None),
            P("fsdp"),
            P("fsdp", None),
            P("fsdp"),
            P("fsdp", None),
            P("fsdp", None),
            P(None, "fsdp", None),
            P(None, "fsdp", None),
        ),
        check_vma=False,
    )
```

profile of v0, /device:TPU:0, one launch (start us, length us, event | category | flops | bytes accessed | tf_op | source)
XLA Modules:
  0.0 1293.1 jit_solution(14940103486952352662)
XLA Ops:
  14.9 27.1 %all-gather.6.cloned.1.call-done.refs_1_.refs_5_ = bf16[2048,512]{1,0:T(8,128)(2,1)} async-done(((bf16[256,512]{1,0:T(8,128)(2,1)}), bf16[2048,512]{1,0:T(8,128)(2,1)}) %all-gather.6.cloned.1.call-update) | async-done | bytes 2097168 | tf_op jit(solution)/shard_map/all_gather | solution.py:691
  45.1 67.7 %all-gather.8.cloned.1.call-done.refs_2_.refs_1_ = bf16[2048,1664]{1,0:T(8,128)(2,1)} async-done(((bf16[256,1664]{1,0:T(8,128)(2,1)}), bf16[2048,1664]{1,0:T(8,128)(2,1)}) %all-gather.8.cloned.1.call-update) | async-done | bytes 6815760 | tf_op jit(solution)/shard_map/all_gather | solution.py:691
  182.6 43.8 %collective-permute-done.4.refs_6_.refs_3_ = bf16[2048,512]{1,0:T(8,128)(2,1)S(1)} collective-permute-done((bf16[2048,512]{1,0:T(8,128)(2,1)S(1)}, bf16[2048,512]{1,0:T(8,128)(2,1)S(1)}, u32[]{:S(2)}, u32[]{:S(2)}) %collective-permute-start.4) | collective-permute-done | bytes 2097184 | tf_op jit(solution)/shard_map/ppermute | solution.py:94
  350.9 30.3 %unit_backward.3 = (bf16[1024,1408]{1,0:T(8,128)(2,1)}, bf16[1024,2816]{1,0:T(8,128)(2,1)}, f32[1024,1]{1,0:T(8,128)}) custom-call(bf16[1024,2048]{1,0:T(8,128)(2,1)} %copy-done.5, bf16[1024,2048]{1,0:T(8,128)(2,1)} %copy-done.52, bf16[2048,4224]{1,0:T(8,128)(2,1)} %all-gather.14.cloned.1.call-done.refs_2_.refs_1_.refs_3_, f32[1024,1]{1,0:T(8,128)} %add_divide_fusion.refs_3_), custom_call_target="tpu_custom_call" | custom-call | flops 17716740096 | bytes 34349056 | tf_op jit(solution)/shard_map/unit_backward/pallas_call | solution.py:182
  381.1 25.4 %grad_matmul.5.refs_4_ = bf16[2048,4224]{1,0:T(8,128)(2,1)} custom-call(bf16[1024,2048]{1,0:T(8,128)(2,1)} %copy-done.5, bf16[1024,2816]{1,0:T(8,128)(2,1)} %get-tuple-element.38.refs_1_.refs_0_, bf16[1024,2048]{1,0:T(8,128)(2,1)} %copy-done.52, bf16[1024,1408]{1,0:T(8,128)(2,1)} %get-tuple-element.39.refs_3_.refs_4_.refs_2_, ...), custom_call_target="tpu_custom_call" | custom-call | flops 17716740096 | bytes 34340864 | tf_op jit(solution)/shard_map/grad_matmul/pallas_call | solution.py:182
  414.9 26.1 %back_matmul.6 = (f32[1024,2048]{1,0:T(8,128)}, f32[1024,2048]{1,0:T(8,128)}) custom-call(bf16[1024,2816]{1,0:T(8,128)(2,1)} %get-tuple-element.38.refs_1_.refs_0_, bf16[2048,4224]{1,0:T(8,128)(2,1)} %all-gather.14.cloned.1.call-done.refs_2_.refs_1_.refs_3_, bf16[1024,1408]{1,0:T(8,128)(2,1)} %get-tuple-element.39.refs_3_.refs_4_.refs_2_, ...), custom_call_target="tpu_custom_call" | custom-call | flops 17716740096 | bytes 60030976 | tf_op jit(solution)/shard_map/back_matmul/pallas_call | solution.py:182
  441.0 30.0 %unit_backward.4 = (bf16[1024,1408]{1,0:T(8,128)(2,1)}, bf16[1024,2816]{1,0:T(8,128)(2,1)}, f32[1024,1]{1,0:T(8,128)}) custom-call(bf16[1024,2048]{1,0:T(8,128)(2,1)} %copy-done.5, bf16[1024,2048]{1,0:T(8,128)(2,1)} %copy-done.52, bf16[2048,4224]{1,0:T(8,128)(2,1)} %all-gather.12.cloned.1.call-done.refs_2_.refs_1_.refs_4_, f32[1024,1]{1,0:T(8,128)} %copy.92.refs_3_, ...), custom_call_target="tpu_custom_call" | custom-call | flops 17716740096 | bytes 34349056 | tf_op jit(solution)/shard_map/unit_backward/pallas_call | solution.py:182
  471.0 25.5 %grad_matmul.6.refs_6_ = bf16[2048,4224]{1,0:T(8,128)(2,1)} custom-call(bf16[1024,2048]{1,0:T(8,128)(2,1)} %copy-done.5, bf16[1024,2816]{1,0:T(8,128)(2,1)} %get-tuple-element.41.refs_1_.refs_0_, bf16[1024,2048]{1,0:T(8,128)(2,1)} %copy-done.52, bf16[1024,1408]{1,0:T(8,128)(2,1)} %get-tuple-element.42.refs_3_.refs_4_, ...), custom_call_target="tpu_custom_call" | custom-call | flops 17716740096 | bytes 34340864 | tf_op jit(solution)/shard_map/grad_matmul/pallas_call | solution.py:182
  500.8 29.0 %back_matmul.7 = (f32[1024,2048]{1,0:T(8,128)}, f32[1024,2048]{1,0:T(8,128)}) custom-call(bf16[1024,2816]{1,0:T(8,128)(2,1)} %get-tuple-element.41.refs_1_.refs_0_, bf16[2048,4224]{1,0:T(8,128)(2,1)} %all-gather.12.cloned.1.call-done.refs_2_.refs_1_.refs_4_, f32[1024,2048]{1,0:T(8,128)} %get-tuple-element.40.refs_4_.refs_2_, ...), custom_call_target="tpu_custom_call" | custom-call | flops 17716740096 | bytes 76808192 | tf_op jit(solution)/shard_map/back_matmul/pallas_call | solution.py:182
  529.7 49.7 %all-gather.10.cloned.1.call-done.refs_2_.refs_1_ = bf16[2048,4224]{1,0:T(8,128)(2,1)} async-done(((bf16[256,4224]{1,0:T(8,128)(2,1)}), bf16[2048,4224]{1,0:T(8,128)(2,1)}) %all-gather.10.cloned.1.call-update) | async-done | bytes 17301520 | tf_op jit(solution)/shard_map/all_gather | solution.py:691
  579.5 30.0 %unit_backward.5 = (bf16[1024,1408]{1,0:T(8,128)(2,1)}, bf16[1024,2816]{1,0:T(8,128)(2,1)}, f32[1024,1]{1,0:T(8,128)}) custom-call(bf16[1024,2048]{1,0:T(8,128)(2,1)} %copy-done.5, bf16[1024,2048]{1,0:T(8,128)(2,1)} %copy-done.52, bf16[2048,4224]{1,0:T(8,128)(2,1)} %all-gather.10.cloned.1.call-done.refs_2_.refs_1_, f32[1024,1]{1,0:T(8,128)} %copy.93.refs_3_, ...), custom_call_target="tpu_custom_call" | custom-call | flops 17716740096 | bytes 34349056 | tf_op jit(solution)/shard_map/unit_backward/pallas_call | solution.py:182
  611.8 19.2 %back_matmul.8.refs_4_ = bf16[1024,2048]{1,0:T(8,128)(2,1)} custom-call(bf16[1024,2816]{1,0:T(8,128)(2,1)} %get-tuple-element.47.refs_0_.refs_1_, bf16[2048,4224]{1,0:T(8,128)(2,1)} %all-gather.10.cloned.1.call-done.refs_2_.refs_1_, bf16[1024,18]{1,0:T(8,128)(2,1)} %copy.96.refs_2_, bf16[2048,18]{1,0:T(8,128)(2,1)} %pad_maximum_fusion.20.refs_3_, ...), custom_call_target="tpu_custom_call" | custom-call | flops 11886657536 | bytes 35762176 | tf_op jit(solution)/shard_map/back_matmul/pallas_call | solution.py:182
  631.0 25.5 %grad_matmul.7.refs_3_ = bf16[2048,4224]{1,0:T(8,128)(2,1)} custom-call(bf16[1024,2048]{1,0:T(8,128)(2,1)} %copy-done.5, bf16[1024,2816]{1,0:T(8,128)(2,1)} %get-tuple-element.47.refs_0_.refs_1_, bf16[1024,2048]{1,0:T(8,128)(2,1)} %copy-done.52, bf16[1024,1408]{1,0:T(8,128)(2,1)} %get-tuple-element.45.refs_5_.refs_3_.refs_0_, ...), custom_call_target="tpu_custom_call" | custom-call | flops 17716740096 | bytes 34340864 | tf_op jit(solution)/shard_map/grad_matmul/pallas_call | solution.py:182
  661.5 22.5 %collective-permute-done.24 = bf16[256,2048]{1,0:T(8,128)(2,1)S(1)} collective-permute-done((bf16[256,2048]{1,0:T(8,128)(2,1)S(1)}, bf16[256,2048]{1,0:T(8,128)(2,1)S(1)}, u32[]{:S(2)}, u32[]{:S(2)}) %collective-permute-start.24) | collective-permute-done | bytes 1048608 | tf_op jit(solution)/shard_map/ppermute | solution.py:94
  734.4 21.1 %attend_back.1.refs_1_.refs_0_ = bf16[1024,1536]{1,0:T(8,128)(2,1)} custom-call(bf16[1024,1536]{1,0:T(8,128)(2,1)} %get-tuple-element.36.refs_0_.refs_1_.refs_2_, bf16[1024,1536]{1,0:T(8,128)(2,1)} %get-tuple-element.36.refs_0_.refs_1_.refs_2_, bf16[1024,1536]{1,0:T(8,128)(2,1)} %get-tuple-element.36.refs_0_.refs_1_.refs_2_, s32[1024,1]{1,0:T(8,128)} %copy.86.refs_3_, ...), custom_call_target="tpu_custom_call" | custom-call | flops 5368709120 | bytes 14704640 | tf_op jit(solution)/shard_map/attend_back/pallas_call | solution.py:182
  828.0 38.0 %collective-permute-done.69 = f32[20480]{0:T(1024)S(1)} collective-permute-done((f32[20480]{0:T(1024)S(1)}, f32[20480]{0:T(1024)S(1)}, u32[]{:S(2)}, u32[]{:S(2)}) %collective-permute-start.69) | collective-permute-done | bytes 81952 | tf_op jit(solution)/shard_map/ppermute | solution.py:94
  868.6 42.7 %collective-permute-done.40 = f32[8192]{0:T(1024)S(1)} collective-permute-done((f32[8192]{0:T(1024)S(1)}, f32[8192]{0:T(1024)S(1)}, u32[]{:S(2)}, u32[]{:S(2)}) %collective-permute-start.40) | collective-permute-done | bytes 32800 | tf_op jit(solution)/shard_map/ppermute | solution.py:94
  951.3 17.4 %collective-permute-done.31 = bf16[256,2048]{1,0:T(8,128)(2,1)} collective-permute-done((bf16[256,2048]{1,0:T(8,128)(2,1)}, bf16[256,2048]{1,0:T(8,128)(2,1)}, u32[]{:S(2)}, u32[]{:S(2)}) %collective-permute-start.31) | collective-permute-done | bytes 1048608 | tf_op jit(solution)/shard_map/ppermute | solution.py:94
  973.8 17.3 %collective-permute-done.59 = bf16[1024,512]{1,0:T(8,128)(2,1)S(1)} collective-permute-done((bf16[1024,512]{1,0:T(8,128)(2,1)S(1)}, bf16[1024,512]{1,0:T(8,128)(2,1)S(1)}, u32[]{:S(2)}, u32[]{:S(2)}) %collective-permute-start.59) | collective-permute-done | bytes 1048608 | tf_op jit(solution)/shard_map/ppermute | solution.py:94
  994.9 19.4 %collective-permute-done.48 = bf16[128,4224]{1,0:T(8,128)(2,1)S(1)} collective-permute-done((bf16[128,4224]{1,0:T(8,128)(2,1)S(1)}, bf16[128,4224]{1,0:T(8,128)(2,1)S(1)}, u32[]{:S(2)}, u32[]{:S(2)}) %collective-permute-start.48) | collective-permute-done | bytes 1081376 | tf_op jit(solution)/shard_map/ppermute | solution.py:94
  1015.8 23.9 %place_grads.3 = (f32[256,11264]{1,0:T(8,128)}, f32[256,5632]{1,0:T(8,128)}) custom-call(s32[1]{0:T(128)} %bitcast.15.refs_0_, bf16[256,4224]{1,0:T(8,128)(2,1)} %after.16.refs_1_, bf16[256,4224]{1,0:T(8,128)(2,1)} %collective-permute-done.46.refs_2_, bf16[256,4224]{1,0:T(8,128)(2,1)} %collective-permute-done.47.refs_3_, ...), custom_call_target="tpu_custom_call" | custom-call | bytes 25952256 | tf_op jit(solution)/shard_map/place_grads/pallas_call | solution.py:182
  1042.0 64.5 %reduce-scatter.8.cloned.1.call-done.refs_0_ = bf16[256,4224]{1,0:T(8,128)(2,1)} async-done(((bf16[2048,4224]{1,0:T(8,128)(2,1)}), bf16[256,4224]{1,0:T(8,128)(2,1)}) %reduce-scatter.8.cloned.1.call-update) | async-done | bytes 2162704 | tf_op jit(solution)/shard_map/reduce_scatter | solution.py:694
  1124.0 53.5 %reduce-scatter.6.cloned.1.call-done.refs_1_ = bf16[256,1536]{1,0:T(8,128)(2,1)} async-done(((bf16[2048,1536]{1,0:T(8,128)(2,1)}), bf16[256,1536]{1,0:T(8,128)(2,1)}) %reduce-scatter.6.cloned.1.call-update) | async-done | bytes 786448 | tf_op jit(solution)/shard_map/reduce_scatter | solution.py:694
  1202.1 22.2 %collective-permute-done.42.refs_2_ = bf16[256,1536]{1,0:T(8,128)(2,1)S(1)} collective-permute-done((bf16[256,1536]{1,0:T(8,128)(2,1)S(1)}, bf16[256,1536]{1,0:T(8,128)(2,1)S(1)}, u32[]{:S(2)}, u32[]{:S(2)}) %collective-permute-start.42) | collective-permute-done | bytes 786464 | tf_op jit(solution)/shard_map/ppermute | solution.py:94
  (486 shorter events, 505.6 us)
Async XLA Ops:
  9.1 103.8 %all-gather.8.cloned.1.call-start = ((), (), s32[]{:S(2)}) async-start(), calls=%async_computation.6 | async-start | bytes 7667712 | tf_op jit(solution)/shard_map/all_gather | solution.py:691
  42.1 308.8 %all-gather.14.cloned.1.call-start = ((), (), s32[]{:S(2)}) async-start(), calls=%async_computation.9 | async-start | bytes 19464192 | tf_op jit(solution)/shard_map/all_gather | solution.py:691
  112.9 328.1 %all-gather.12.cloned.1.call-start = ((), (), s32[]{:S(2)}) async-start(), calls=%async_computation.8 | async-start | bytes 19464192 | tf_op jit(solution)/shard_map/all_gather | solution.py:691
  179.1 400.4 %all-gather.10.cloned.1.call-start = ((), (), s32[]{:S(2)}) async-start(), calls=%async_computation.7 | async-start | bytes 19464192 | tf_op jit(solution)/shard_map/all_gather | solution.py:691
  267.7 543.7 %reduce-scatter.10.cloned.1.call-start = ((), (), s32[]{:S(2)}) async-start(), calls=%async_computation.12 | async-start | bytes 19464192 | tf_op jit(solution)/shard_map/reduce_scatter | solution.py:694
  406.6 633.1 %reduce-scatter.12.cloned.1.call-start = ((), (), s32[]{:S(2)}) async-start(), calls=%async_computation.13 | async-start | bytes 19464192 | tf_op jit(solution)/shard_map/reduce_scatter | solution.py:694
  496.5 609.9 %reduce-scatter.8.cloned.1.call-start = ((), (), s32[]{:S(2)}) async-start(), calls=%async_computation.11 | async-start | bytes 19464192 | tf_op jit(solution)/shard_map/reduce_scatter | solution.py:694
  656.6 521.0 %reduce-scatter.6.cloned.1.call-start = ((), (), s32[]{:S(2)}) async-start(), calls=%async_computation.10 | async-start | bytes 7077888 | tf_op jit(solution)/shard_map/reduce_scatter | solution.py:694
  767.8 495.8 %reduce-scatter.14.cloned.1.call-start = ((), (), s32[]{:S(2)}) async-start(), calls=%async_computation.14 | async-start | bytes 2359296 | tf_op jit(solution)/shard_map/reduce_scatter | solution.py:694
  808.3 112.5 %collective-permute-start.60 = (bf16[2048,512]{1,0:T(8,128)(2,1)}, bf16[2048,512]{1,0:T(8,128)(2,1)}, u32[]{:S(2)}, u32[]{:S(2)}) collective-permute-start(bf16[2048,512]{1,0:T(8,128)(2,1)} %pad_maximum_fusion.7), channel_id=1, source_target_pairs={{0,16},{8,24},{16,0},{24,8},{1,17},{9,25},{17,1},{25,9},{2,18},{10... | collective-permute-start | bytes 6291464 | tf_op jit(solution)/shard_map/ppermute | solution.py:94
  811.4 113.5 %collective-permute-start.47 = (bf16[256,4224]{1,0:T(8,128)(2,1)}, bf16[256,4224]{1,0:T(8,128)(2,1)}, u32[]{:S(2)}, u32[]{:S(2)}) collective-permute-start(bf16[256,4224]{1,0:T(8,128)(2,1)} %after.16.refs_1_), channel_id=1, source_target_pairs={{0,16},{8,24},{16,0},{24,8},{1,17},{9,25},{17,1},{25,9},{2,18},{10... | collective-permute-start | bytes 6488072 | tf_op jit(solution)/shard_map/ppermute | solution.py:94
  815.4 108.9 %collective-permute-start.58 = (bf16[2048,512]{1,0:T(8,128)(2,1)}, bf16[2048,512]{1,0:T(8,128)(2,1)}, u32[]{:S(2)}, u32[]{:S(2)}) collective-permute-start(bf16[2048,512]{1,0:T(8,128)(2,1)} %pad_maximum_fusion.6), channel_id=1, source_target_pairs={{0,8},{8,0},{16,24},{24,16},{1,9},{9,1},{17,25},{25,17},{2,10},{10... | collective-permute-start | bytes 6291464 | tf_op jit(solution)/shard_map/ppermute | solution.py:94
  823.7 106.3 %collective-permute-start.46 = (bf16[256,4224]{1,0:T(8,128)(2,1)}, bf16[256,4224]{1,0:T(8,128)(2,1)}, u32[]{:S(2)}, u32[]{:S(2)}) collective-permute-start(bf16[256,4224]{1,0:T(8,128)(2,1)} %after.16.refs_1_), channel_id=1, source_target_pairs={{0,8},{8,0},{16,24},{24,16},{1,9},{9,1},{17,25},{25,17},{2,10},{10... | collective-permute-start | bytes 6488072 | tf_op jit(solution)/shard_map/ppermute | solution.py:94
  930.0 61.1 %collective-permute-start.59 = (bf16[1024,512]{1,0:T(8,128)(2,1)S(1)}, bf16[1024,512]{1,0:T(8,128)(2,1)S(1)}, u32[]{:S(2)}, u32[]{:S(2)}) collective-permute-start(bf16[1024,512]{1,0:T(8,128)(2,1)S(1)} %get-tuple-element.75), channel_id=1, source_target_pairs={{0,16},{8,24},{16,0},{24,8},{1,17},{9,25},{17,1},{25,9},{2,18},{10... | collective-permute-start | bytes 3145736 | tf_op jit(solution)/shard_map/ppermute | solution.py:94
  947.2 67.0 %collective-permute-start.48 = (bf16[128,4224]{1,0:T(8,128)(2,1)S(1)}, bf16[128,4224]{1,0:T(8,128)(2,1)S(1)}, u32[]{:S(2)}, u32[]{:S(2)}) collective-permute-start(bf16[128,4224]{1,0:T(8,128)(2,1)S(1)} %slice.467), channel_id=1, source_target_pairs={{0,16},{8,24},{16,0},{24,8},{1,17},{9,25},{17,1},{25,9},{2,18},{10... | collective-permute-start | bytes 3244040 | tf_op jit(solution)/shard_map/ppermute | solution.py:94
  968.7 141.1 %collective-permute-start.34 = (bf16[128,2048]{1,0:T(8,128)(2,1)}, bf16[128,2048]{1,0:T(8,128)(2,1)}, u32[]{:S(2)}, u32[]{:S(2)}) collective-permute-start(bf16[128,2048]{1,0:T(8,128)(2,1)} %get-tuple-element.85), channel_id=1, source_target_pairs={{0,16},{8,24},{16,0},{24,8},{1,17},{9,25},{17,1},{25,9},{2,18},{10... | collective-permute-start | bytes 1572872 | tf_op jit(solution)/shard_map/ppermute | solution.py:94
  969.7 136.8 %collective-permute-start.61 = (bf16[1024,512]{1,0:T(8,128)(2,1)}, bf16[1024,512]{1,0:T(8,128)(2,1)}, u32[]{:S(2)}, u32[]{:S(2)}) collective-permute-start(bf16[1024,512]{1,0:T(8,128)(2,1)} %get-tuple-element.76), channel_id=1, source_target_pairs={{0,8},{8,0},{16,24},{24,16},{1,9},{9,1},{17,25},{25,17},{2,10},{10... | collective-permute-start | bytes 3145736 | tf_op jit(solution)/shard_map/ppermute | solution.py:94
  991.1 125.4 %collective-permute-start.36 = (bf16[128,2048]{1,0:T(8,128)(2,1)S(1)}, bf16[128,2048]{1,0:T(8,128)(2,1)}, u32[]{:S(2)}, u32[]{:S(2)}) collective-permute-start(bf16[128,2048]{1,0:T(8,128)(2,1)S(1)} %get-tuple-element.86), channel_id=1, source_target_pairs={{0,8},{8,0},{16,24},{24,16},{1,9},{9,1},{17,25},{25,17},{2,10},{10... | collective-permute-start | bytes 1572872 | tf_op jit(solution)/shard_map/ppermute | solution.py:94
  1039.7 81.2 %collective-permute-start.55 = (bf16[256,4224]{1,0:T(8,128)(2,1)}, bf16[256,4224]{1,0:T(8,128)(2,1)}, u32[]{:S(2)}, u32[]{:S(2)}) collective-permute-start(bf16[256,4224]{1,0:T(8,128)(2,1)} %after.18.refs_1_), channel_id=1, source_target_pairs={{0,16},{8,24},{16,0},{24,8},{1,17},{9,25},{17,1},{25,9},{2,18},{10... | collective-permute-start | bytes 6488072 | tf_op jit(solution)/shard_map/ppermute | solution.py:94
  1040.7 136.9 %collective-permute-start.54 = (bf16[256,4224]{1,0:T(8,128)(2,1)}, bf16[256,4224]{1,0:T(8,128)(2,1)}, u32[]{:S(2)}, u32[]{:S(2)}) collective-permute-start(bf16[256,4224]{1,0:T(8,128)(2,1)} %after.18.refs_1_), channel_id=1, source_target_pairs={{0,8},{8,0},{16,24},{24,16},{1,9},{9,1},{17,25},{25,17},{2,10},{10... | collective-permute-start | bytes 6488072 | tf_op jit(solution)/shard_map/ppermute | solution.py:94
  1106.5 75.4 %collective-permute-start.51 = (bf16[256,4224]{1,0:T(8,128)(2,1)}, bf16[256,4224]{1,0:T(8,128)(2,1)}, u32[]{:S(2)}, u32[]{:S(2)}) collective-permute-start(bf16[256,4224]{1,0:T(8,128)(2,1)} %after.17.refs_1_), channel_id=1, source_target_pairs={{0,16},{8,24},{16,0},{24,8},{1,17},{9,25},{17,1},{25,9},{2,18},{10... | collective-permute-start | bytes 6488072 | tf_op jit(solution)/shard_map/ppermute | solution.py:94
  1109.8 77.1 %collective-permute-start.50 = (bf16[256,4224]{1,0:T(8,128)(2,1)}, bf16[256,4224]{1,0:T(8,128)(2,1)}, u32[]{:S(2)}, u32[]{:S(2)}) collective-permute-start(bf16[256,4224]{1,0:T(8,128)(2,1)} %after.17.refs_1_), channel_id=1, source_target_pairs={{0,8},{8,0},{16,24},{24,16},{1,9},{9,1},{17,25},{25,17},{2,10},{10... | collective-permute-start | bytes 6488072 | tf_op jit(solution)/shard_map/ppermute | solution.py:94
  1116.5 63.8 %collective-permute-start.30 = (bf16[128,2048]{1,0:T(8,128)(2,1)}, bf16[128,2048]{1,0:T(8,128)(2,1)}, u32[]{:S(2)}, u32[]{:S(2)}) collective-permute-start(bf16[128,2048]{1,0:T(8,128)(2,1)} %get-tuple-element.91), channel_id=1, source_target_pairs={{0,16},{8,24},{16,0},{24,8},{1,17},{9,25},{17,1},{25,9},{2,18},{10... | collective-permute-start | bytes 1572872 | tf_op jit(solution)/shard_map/ppermute | solution.py:94
  1120.9 71.4 %collective-permute-start.32 = (bf16[128,2048]{1,0:T(8,128)(2,1)S(1)}, bf16[128,2048]{1,0:T(8,128)(2,1)}, u32[]{:S(2)}, u32[]{:S(2)}) collective-permute-start(bf16[128,2048]{1,0:T(8,128)(2,1)S(1)} %get-tuple-element.92), channel_id=1, source_target_pairs={{0,8},{8,0},{16,24},{24,16},{1,9},{9,1},{17,25},{25,17},{2,10},{10... | collective-permute-start | bytes 1572872 | tf_op jit(solution)/shard_map/ppermute | solution.py:94
  (119 other events, 2130.9 us)
Sparse Core Ops, SparseCore 0:
  10.2 31.7 all-gather.5
  44.3 68.5 all-gather.7
  115.1 154.0 all-gather.13
  270.6 153.6 all-gather.11
  425.8 153.6 all-gather.9
  582.3 171.3 reduce-scatter.9
  756.1 176.4 reduce-scatter.11
  934.9 171.5 reduce-scatter.7
  1109.4 68.1 reduce-scatter.5
  1180.3 34.0 reduce-scatter.13
where the time goes:
time: 1300 us; the launch traced here: 1290 us
  waiting for transfers between devices  602 us (46%)
  Pallas kernels  409 us (31%)
  other arithmetic  94.1 us (7%)
  local copies, waits for them, and re-layouts  84 us (6%)
  starting transfers between devices  82.1 us (6%)
  between operations  15.6 us (1%)
    pallas_call x21, Pallas kernels, own_call(): pl.pallas_call(body, out_shape=list(outs), grid_spec=pltpu.PrefetchScalar...  409 us
    ppermute x65, waiting for transfers between devices, to_peer(): lax.ppermute(array, 'ctx', [(rank, rank ^ bits) for rank in range(size)])  338 us
    all_gather x5, waiting for transfers between devices, gather_fsdp(): return lax.all_gather(array, 'fsdp', axis=0, tiled=True)  145 us
    reduce_scatter x5, waiting for transfers between devices, scatter_fsdp(): lax.psum_scatter(array.astype(jnp.bfloat16), 'fsdp', scatter_dimension=0,...  118 us
    ppermute x65, starting transfers between devices, to_peer(): lax.ppermute(array, 'ctx', [(rank, rank ^ bits) for rank in range(size)])  74.4 us
    unnamed x140, local copies, waits for them, and re-layouts  26.6 us
  transfers between devices with their start and end apart: 81, of which 40 were waited for; matrix products, arithmetic and copies ran while one was open for 13% of the time, Pallas kernels for 32%

commit v1 on v0

--- a/solution.py
+++ b/solution.py
@@ -324,20 +324,25 @@
     return (jnp.concatenate([coarse, fine], axis=1), both, 0)
 
 
-def grad_matmul(pairs, waits=()):
+def grad_matmul(pairs, waits=(), core=None, add=None):
     blocks = lax.axis_size("fsdp")
     depth = pairs[0][0][0].shape[1]
     widths = [rights[0].shape[1] for lefts, rights in pairs]
     total, block = sum(widths), depth // blocks
+    step, first = (1, 0) if core is None else (2, core)
+    blocks //= step
     ins, specs, flops = [], [], 0
     for lefts, rights in pairs:
         for left, right in zip(lefts, rights):
             ins += [left, right]
             specs += [
-                pl.BlockSpec((left.shape[0], block), lambda j: (0, j)),
-                pl.BlockSpec(right.shape, lambda j: (0, 0)),
+                pl.BlockSpec((left.shape[0], block), lambda j, first_ref: (0, step * j + first_ref[0])),
+                pl.BlockSpec(right.shape, lambda j, first_ref: (0, 0)),
             ]
-            flops += 2 * left.shape[0] * depth * right.shape[1]
+            flops += 2 * left.shape[0] * depth // step * right.shape[1]
+    if add is not None:
+        ins.append(add)
+        specs.append(pl.BlockSpec((block, total), lambda j, first_ref: (j, 0)))
 
     def kernel(*refs):
         start, used = 0, 0
@@ -352,6 +357,8 @@
                 )
                 value = part if value is None else value + part
                 used += 2
+            if add is not None:
+                value = value + wide(refs[-2][:, start : start + width])
             refs[-1][:, start : start + width] = low(value)
             start += width
 
@@ -361,10 +368,11 @@
         (blocks,),
         ins,
         specs,
-        [jax.ShapeDtypeStruct((depth, total), jnp.bfloat16)],
-        [pl.BlockSpec((block, total), lambda j: (j, 0))],
+        [jax.ShapeDtypeStruct((blocks * block, total), jnp.bfloat16)],
+        [pl.BlockSpec((block, total), lambda j, first_ref: (j, 0))],
         flops,
         waits,
+        jnp.asarray(first, jnp.int32).reshape(1),
     )[0]
 
 
@@ -545,16 +553,17 @@
             for k in range(3)
         ]
         into = jnp.stack(sides[:2], axis=1).reshape(rows, 2 * size * units)
-        return wide(into), wide(sides[2].reshape(rows, size * units))
+        return wide(into), wide(sides[2].reshape(rows, size * units)), spread[0][0][0]
     tall = min(rows, 64)
     columns = 2 if slot is None else 1
     pieces = [held[k] for k in range(size) for held, parts in spread]
-    onto = [] if totals is None else list(totals)
+    onto = [] if totals is None else list(totals[:2])
     rest = list(waits) + onto
     steps = rows // tall
 
     def kernel(*refs):
-        in_ref, out_ref = refs[-2:]
+        in_ref, out_ref, mark_ref = refs[-3:]
+        mark_ref[...] = jnp.zeros_like(mark_ref)
         for k in range(size):
 
             @pl.when(pl.program_id(0) == k)
@@ -609,8 +618,8 @@
         (size, steps, columns),
         pieces,
         [piece_spec(k, parts) for k in range(size) for held, parts in spread],
-        [jax.ShapeDtypeStruct(shape, jnp.float32) for shape in shapes],
-        out_specs,
+        [jax.ShapeDtypeStruct(shape, jnp.float32) for shape in [*shapes, (8, 128)]],
+        out_specs + [pl.BlockSpec((8, 128), lambda k, row, column, rank_ref: (0, 0))],
         0,
         rest,
         lax.axis_index("ctx").reshape(1),
@@ -719,6 +728,14 @@
     bias_full = jnp.transpose(bias_full, (0, 2, 1)).reshape(3, D)
     bias_own = wide(own_cols(bias_full, 0, att_cols)).reshape(3 * att_cols)
 
+    core = fsdp_rank % 2
+    lines = [[rank for rank in range(fsdp_size) if rank % 2 == spot] for spot in range(2)]
+
+    def scatter_line(grad):
+        return lax.psum_scatter(
+            grad, "fsdp", scatter_dimension=0, axis_index_groups=lines, tiled=True
+        )
+
     slabs = [
         [own_cols(w_sh_in, part * FS, sh_cols) for part in range(2)]
         + [own_cols(w_sh_out, 0, sh_cols)]
@@ -797,16 +814,20 @@
             products.append(route_product(d_route, route_mat))
             d_hidden_sum = back_matmul([(products, sums[0], jnp.bfloat16)], waits)[0]
             waits = [d_hidden_sum]
-        grads.append(grad_matmul([(hidden, [d_act]), (cots, [scaled_out])], waits))
-        waits = [grads[-1]]
+        pairs = [(hidden, [d_act]), (cots, [scaled_out])]
+        given = grad_matmul(pairs, waits, 1 - core)
+        waits = [given]
         if index < len(weights) - 1:
             sums = back_matmul(
                 [(products, sums[0], jnp.float32), (outward, sums[1], jnp.float32)], waits
             )
             waits = [sums[0]]
-    block_sum = back_matmul([(outward, sums[1], jnp.bfloat16)], waits)[0]
-    waits = [block_sum]
-    shards = [scatter_fsdp(grad) for grad in grads]
+        else:
+            block_sum = back_matmul([(outward, sums[1], jnp.bfloat16)], waits)[0]
+            waits = [block_sum]
+        grads.append(grad_matmul(pairs, waits, core, to_mate(given, 1)))
+        waits = [grads[-1]]
+    shards = [scatter_line(grad) for grad in grads]
     d_route_mat = lax.dot_general(
         d_route,
         wide(hidden[0]),
@@ -839,12 +860,14 @@
     )
     grad_w_out = scatter_fsdp(grad_w_out)
     d_mixed = attend_back(split, places, log_total, d_vec, cos_table, sin_table, heads_own)
-    grad_w_in = grad_matmul([([normed_all], [d_mixed])])
+    given = grad_matmul([([normed_all], [d_mixed])], (), 1 - core)
     d_bias = jnp.sum(wide(d_mixed), axis=0)
     d_normed_part = back_matmul(
-        [([(d_mixed, w_in_own, 0)], None, jnp.bfloat16)], [grad_w_in]
+        [([(d_mixed, w_in_own, 0)], None, jnp.bfloat16)], [given]
     )[0]
-    grad_w_in = scatter_fsdp(grad_w_in)
+    grad_w_in = scatter_line(
+        grad_matmul([([normed_all], [d_mixed])], [d_normed_part], core, to_mate(given, 1))
+    )
     d_normed = peer_scatter(token_pieces(d_normed_part))
     block_out = low(residual + peer_scatter(token_pieces(after(block_sum, [d_mixed]))))
     units, totals, waits = [sh_cols] + [FE] * experts_own, None, [d_normed_part]
@@ -852,9 +875,10 @@
         spread = [(peer_gather(after(shard, waits)), units[:1] if own < 0 else units[1:2])]
         if own < 0:
             shared_totals = place_grads(spread, None, 1, None, waits)
-            waits = [shared_totals[0]]
+            waits = [shared_totals[2]]
         else:
             totals = place_grads(spread, own, experts_own, totals, waits)
+            waits = [totals[2]]
     wide_all = wide(tokens_all)
     d_gain_one = jnp.sum(wide(d_normed_part) * (wide_all * rms_scale(wide_all)), axis=0)
     d_tokens = d_resid + rms_back(d_normed, unit_one, scale_one, gain_one)
@@ -877,12 +901,12 @@
         own_part(late_grads[3 * D :]),
         place_cols(peer_gather(grad_w_in), 3, [totals[1]]),
         own_part(late_grads[: 3 * D]),
-        wide(jnp.concatenate(by_rank(peer_gather(after(grad_w_out, totals[:1]))), axis=1)),
+        wide(jnp.concatenate(by_rank(peer_gather(grad_w_out)), axis=1)),
         own_part(early_grads[(EXPERTS + 1) * D :]),
         route_part[:EXPERTS].T,
         route_part[EXPERTS],
-        *shared_totals,
-        *totals,
+        *shared_totals[:2],
+        *totals[:2],
     )
 
 

time: 1300 us -> 1270 us (0.977)
  waiting for transfers between devices: 602 us -> 560 us
  Pallas kernels: 409 us -> 432 us
    reduce_scatter x5 -> x1, waiting for transfers between devices: 118 us -> 0.01 us  [scatter_fsdp(): lax.psum_scatter(array.astype(jnp.bfloat16), 'fsdp', scatter_dimension=0,...]
    ppermute x65, waiting for transfers between devices: 338 us -> 407 us  [to_peer(): lax.ppermute(array, 'ctx', [(rank, rank ^ bits) for rank in range(size)])]
    pallas_call x21 -> x25, Pallas kernels: 409 us -> 432 us  [own_call(): pl.pallas_call(body, out_shape=list(outs), grid_spec=pltpu.PrefetchScalar...]
    ppermute x6 -> x10, waiting for transfers between devices: 2 us -> 22.5 us  [to_mate(): lax.ppermute(array, 'fsdp', [(rank, rank ^ bits) for rank in range(size)])]
    all_gather x5, waiting for transfers between devices: 145 us -> 130 us  [gather_fsdp(): return lax.all_gather(array, 'fsdp', axis=0, tiled=True)]
    unnamed x140 -> x126, local copies, waits for them, and re-layouts: 26.6 us -> 26 us
  transfers between devices with their start and end apart: 81 -> 85, of which waited for: 40 -> 40; matrix products, arithmetic and copies ran while one was open for 13% -> 12% of each run, Pallas kernels for 32% -> 33%
where the time goes in v1:
time: 1270 us; the launch traced here: 1250 us
  waiting for transfers between devices  560 us (44%)
  Pallas kernels  432 us (34%)
  other arithmetic  82.8 us (7%)
  local copies, waits for them, and re-layouts  79.2 us (6%)
  starting transfers between devices  78.3 us (6%)
  between operations  15.6 us (1%)
    pallas_call x25, Pallas kernels, own_call(): pl.pallas_call(body, out_shape=list(outs), grid_spec=pltpu.PrefetchScalar...  432 us
    ppermute x65, waiting for transfers between devices, to_peer(): lax.ppermute(array, 'ctx', [(rank, rank ^ bits) for rank in range(size)])  407 us
    all_gather x5, waiting for transfers between devices, gather_fsdp(): return lax.all_gather(array, 'fsdp', axis=0, tiled=True)  130 us
    ppermute x65, starting transfers between devices, to_peer(): lax.ppermute(array, 'ctx', [(rank, rank ^ bits) for rank in range(size)])  75.5 us
    unnamed x126, local copies, waits for them, and re-layouts  26 us
  transfers between devices with their start and end apart: 85, of which 40 were waited for; matrix products, arithmetic and copies ran while one was open for 12% of the time, Pallas kernels for 33%

profile of v1, /device:TPU:0, one launch (start us, length us, event | category | flops | bytes accessed | tf_op | source)
XLA Modules:
  0.0 1253.4 jit_solution(1381596534883768370)
XLA Ops:
  14.9 27.1 %all-gather.6.cloned.1.call-done.refs_1_.refs_5_ = bf16[2048,512]{1,0:T(8,128)(2,1)} async-done(((bf16[256,512]{1,0:T(8,128)(2,1)}), bf16[2048,512]{1,0:T(8,128)(2,1)}) %all-gather.6.cloned.1.call-update) | async-done | bytes 2097168 | tf_op jit(solution)/shard_map/all_gather | solution.py:700
  45.1 67.7 %all-gather.8.cloned.1.call-done.refs_2_.refs_1_ = bf16[2048,1664]{1,0:T(8,128)(2,1)} async-done(((bf16[256,1664]{1,0:T(8,128)(2,1)}), bf16[2048,1664]{1,0:T(8,128)(2,1)}) %all-gather.8.cloned.1.call-update) | async-done | bytes 6815760 | tf_op jit(solution)/shard_map/all_gather | solution.py:700
  162.9 16.0 %split_matmul.1 = (bf16[1024,2048]{1,0:T(8,128)(2,1)}, bf16[1024,1536]{1,0:T(8,128)(2,1)}) custom-call(bf16[1024,2048]{1,0:T(8,128)(2,1)} %constant_dynamic-update-slice_fusion.refs_0_, f32[1,2048]{1,0:T(1,128)} %bitcast.41, bf16[2048,1664]{1,0:T(8,128)(2,1)} %all-gather.8.cloned.1.call-done.refs_2_.refs_1_, f32[1,1536]{1,0:T(1,128)} %bitcast.49, ...), custom_call_target="tpu_custom_call" | custom-call | flops 6442450944 | bytes 19412992 | tf_op jit(solution)/shard_map/split_matmul/pallas_call | solution.py:182
  182.5 43.8 %collective-permute-done.4.refs_6_.refs_3_ = bf16[2048,512]{1,0:T(8,128)(2,1)S(1)} collective-permute-done((bf16[2048,512]{1,0:T(8,128)(2,1)S(1)}, bf16[2048,512]{1,0:T(8,128)(2,1)S(1)}, u32[]{:S(2)}, u32[]{:S(2)}) %collective-permute-start.4) | collective-permute-done | bytes 2097184 | tf_op jit(solution)/shard_map/ppermute | solution.py:94
  234.4 15.7 %collective-permute-done.6 = bf16[1024,512]{1,0:T(8,128)(2,1)} collective-permute-done((bf16[1024,512]{1,0:T(8,128)(2,1)}, bf16[1024,512]{1,0:T(8,128)(2,1)}, u32[]{:S(2)}, u32[]{:S(2)}) %collective-permute-start.6) | collective-permute-done | bytes 1048608 | tf_op jit(solution)/shard_map/ppermute | solution.py:94
  351.7 30.5 %unit_backward.3 = (bf16[1024,1408]{1,0:T(8,128)(2,1)}, bf16[1024,2816]{1,0:T(8,128)(2,1)}, f32[1024,1]{1,0:T(8,128)}) custom-call(bf16[1024,2048]{1,0:T(8,128)(2,1)} %copy-done.3, bf16[1024,2048]{1,0:T(8,128)(2,1)} %copy-done.8, bf16[2048,4224]{1,0:T(8,128)(2,1)} %all-gather.14.cloned.1.call-done.refs_2_.refs_1_.refs_3_, f32[1024,1]{1,0:T(8,128)} %add_divide_fusion.refs_3_), custom_call_target="tpu_custom_call" | custom-call | flops 17716740096 | bytes 34349056 | tf_op jit(solution)/shard_map/unit_backward/pallas_call | solution.py:182
  397.5 25.8 %back_matmul.6 = (f32[1024,2048]{1,0:T(8,128)}, f32[1024,2048]{1,0:T(8,128)}) custom-call(bf16[1024,2816]{1,0:T(8,128)(2,1)} %get-tuple-element.40.refs_2_.refs_0_, bf16[2048,4224]{1,0:T(8,128)(2,1)} %all-gather.14.cloned.1.call-done.refs_2_.refs_1_.refs_3_, bf16[1024,1408]{1,0:T(8,128)(2,1)} %get-tuple-element.41.refs_4_.refs_5_.refs_2_, ...), custom_call_target="tpu_custom_call" | custom-call | flops 17716740096 | bytes 60030976 | tf_op jit(solution)/shard_map/back_matmul/pallas_call | solution.py:182
  423.3 16.8 %grad_matmul.10.refs_4_ = bf16[1024,4224]{1,0:T(8,128)(2,1)} custom-call(s32[1]{0:T(128)} %bitcast.11.refs_0_, bf16[1024,2048]{1,0:T(8,128)(2,1)} %copy-done.3, bf16[1024,2816]{1,0:T(8,128)(2,1)} %get-tuple-element.40.refs_2_.refs_0_, bf16[1024,2048]{1,0:T(8,128)(2,1)} %copy-done.8, bf16[1024,1408]{1,0:T(8,128)(2,1)} %get-tuple-element.41.refs_4_.refs_5_.refs_2_, ...), custom_call_target="tpu_custom_call" | custom-call | flops 8858370048 | bytes 34340864 | tf_op jit(solution)/shard_map/grad_matmul/pallas_call | solution.py:182
  448.9 30.3 %unit_backward.4 = (bf16[1024,1408]{1,0:T(8,128)(2,1)}, bf16[1024,2816]{1,0:T(8,128)(2,1)}, f32[1024,1]{1,0:T(8,128)}) custom-call(bf16[1024,2048]{1,0:T(8,128)(2,1)} %copy-done.3, bf16[1024,2048]{1,0:T(8,128)(2,1)} %copy-done.8, bf16[2048,4224]{1,0:T(8,128)(2,1)} %all-gather.12.cloned.1.call-done.refs_2_.refs_1_.refs_4_, f32[1024,1]{1,0:T(8,128)} %copy.91.refs_3_, ...), custom_call_target="tpu_custom_call" | custom-call | flops 17716740096 | bytes 34349056 | tf_op jit(solution)/shard_map/unit_backward/pallas_call | solution.py:182
  494.5 28.5 %back_matmul.7 = (f32[1024,2048]{1,0:T(8,128)}, f32[1024,2048]{1,0:T(8,128)}) custom-call(bf16[1024,2816]{1,0:T(8,128)(2,1)} %get-tuple-element.43.refs_2_.refs_0_, bf16[2048,4224]{1,0:T(8,128)(2,1)} %all-gather.12.cloned.1.call-done.refs_2_.refs_1_.refs_4_, f32[1024,2048]{1,0:T(8,128)} %get-tuple-element.42.refs_6_.refs_2_, ...), custom_call_target="tpu_custom_call" | custom-call | flops 17716740096 | bytes 76808192 | tf_op jit(solution)/shard_map/back_matmul/pallas_call | solution.py:182
  523.0 16.6 %grad_matmul.12.refs_4_ = bf16[1024,4224]{1,0:T(8,128)(2,1)} custom-call(s32[1]{0:T(128)} %bitcast.11.refs_0_, bf16[1024,2048]{1,0:T(8,128)(2,1)} %copy-done.3, bf16[1024,2816]{1,0:T(8,128)(2,1)} %get-tuple-element.43.refs_2_.refs_0_, bf16[1024,2048]{1,0:T(8,128)(2,1)} %copy-done.8, bf16[1024,1408]{1,0:T(8,128)(2,1)} %get-tuple-element.44.refs_4_.refs_5_.refs_3_, ...), custom_call_target="tpu_custom_call" | custom-call | flops 8858370048 | bytes 34340864 | tf_op jit(solution)/shard_map/grad_matmul/pallas_call | solution.py:182
  543.8 35.6 %all-gather.10.cloned.1.call-done.refs_2_.refs_1_ = bf16[2048,4224]{1,0:T(8,128)(2,1)} async-done(((bf16[256,4224]{1,0:T(8,128)(2,1)}), bf16[2048,4224]{1,0:T(8,128)(2,1)}) %all-gather.10.cloned.1.call-update) | async-done | bytes 17301520 | tf_op jit(solution)/shard_map/all_gather | solution.py:700
  579.5 30.4 %unit_backward.5 = (bf16[1024,1408]{1,0:T(8,128)(2,1)}, bf16[1024,2816]{1,0:T(8,128)(2,1)}, f32[1024,1]{1,0:T(8,128)}) custom-call(bf16[1024,2048]{1,0:T(8,128)(2,1)} %copy-done.3, bf16[1024,2048]{1,0:T(8,128)(2,1)} %copy-done.8, bf16[2048,4224]{1,0:T(8,128)(2,1)} %all-gather.10.cloned.1.call-done.refs_2_.refs_1_, f32[1024,1]{1,0:T(8,128)} %copy.92.refs_3_, ...), custom_call_target="tpu_custom_call" | custom-call | flops 17716740096 | bytes 34349056 | tf_op jit(solution)/shard_map/unit_backward/pallas_call | solution.py:182
  612.2 19.2 %back_matmul.8.refs_5_ = bf16[1024,2048]{1,0:T(8,128)(2,1)} custom-call(bf16[1024,2816]{1,0:T(8,128)(2,1)} %get-tuple-element.49.refs_0_.refs_2_, bf16[2048,4224]{1,0:T(8,128)(2,1)} %all-gather.10.cloned.1.call-done.refs_2_.refs_1_, bf16[1024,18]{1,0:T(8,128)(2,1)} %copy.95.refs_2_, bf16[2048,18]{1,0:T(8,128)(2,1)} %pad_maximum_fusion.20.refs_3_, ...), custom_call_target="tpu_custom_call" | custom-call | flops 11886657536 | bytes 35762176 | tf_op jit(solution)/shard_map/back_matmul/pallas_call | solution.py:182
  661.1 16.4 %grad_matmul.14.refs_8_ = bf16[1024,4224]{1,0:T(8,128)(2,1)} custom-call(s32[1]{0:T(128)} %bitcast.11.refs_0_, bf16[1024,2048]{1,0:T(8,128)(2,1)} %copy-done.3, bf16[1024,2816]{1,0:T(8,128)(2,1)} %get-tuple-element.49.refs_0_.refs_2_, bf16[1024,2048]{1,0:T(8,128)(2,1)} %copy-done.8, bf16[1024,1408]{1,0:T(8,128)(2,1)} %get-tuple-element.47.refs_5_.refs_4_.refs_0_, ...), custom_call_target="tpu_custom_call" | custom-call | flops 8858370048 | bytes 34340864 | tf_op jit(solution)/shard_map/grad_matmul/pallas_call | solution.py:182
  682.8 22.5 %collective-permute-done.26 = bf16[256,2048]{1,0:T(8,128)(2,1)S(1)} collective-permute-done((bf16[256,2048]{1,0:T(8,128)(2,1)S(1)}, bf16[256,2048]{1,0:T(8,128)(2,1)S(1)}, u32[]{:S(2)}, u32[]{:S(2)}) %collective-permute-start.26) | collective-permute-done | bytes 1048608 | tf_op jit(solution)/shard_map/ppermute | solution.py:94
  756.8 38.7 %collective-permute-done.64 = bf16[2048,512]{1,0:T(8,128)(2,1)} collective-permute-done((bf16[2048,512]{1,0:T(8,128)(2,1)}, bf16[2048,512]{1,0:T(8,128)(2,1)}, u32[]{:S(2)}, u32[]{:S(2)}) %collective-permute-start.64) | collective-permute-done | bytes 2097184 | tf_op jit(solution)/shard_map/ppermute | solution.py:94
  808.1 21.1 %attend_back.1.refs_1_.refs_2_.refs_0_ = bf16[1024,1536]{1,0:T(8,128)(2,1)} custom-call(bf16[1024,1536]{1,0:T(8,128)(2,1)} %get-tuple-element.38.refs_0_.refs_1_.refs_2_, bf16[1024,1536]{1,0:T(8,128)(2,1)} %get-tuple-element.38.refs_0_.refs_1_.refs_2_, bf16[1024,1536]{1,0:T(8,128)(2,1)} %get-tuple-element.38.refs_0_.refs_1_.refs_2_, ...), custom_call_target="tpu_custom_call" | custom-call | flops 5368709120 | bytes 14704640 | tf_op jit(solution)/shard_map/attend_back/pallas_call | solution.py:182
  880.3 23.4 %collective-permute-done.73 = f32[20480]{0:T(1024)S(1)} collective-permute-done((f32[20480]{0:T(1024)S(1)}, f32[20480]{0:T(1024)S(1)}, u32[]{:S(2)}, u32[]{:S(2)}) %collective-permute-start.73) | collective-permute-done | bytes 81952 | tf_op jit(solution)/shard_map/ppermute | solution.py:94
  945.4 23.2 %place_grads.3 = (f32[256,11264]{1,0:T(8,128)}, f32[256,5632]{1,0:T(8,128)}, f32[8,128]{1,0:T(8,128)}) custom-call(s32[1]{0:T(128)} %bitcast.17.refs_0_, bf16[256,4224]{1,0:T(8,128)(2,1)} %after.15.refs_1_, bf16[256,4224]{1,0:T(8,128)(2,1)} %collective-permute-done.50.refs_2_, bf16[256,4224]{1,0:T(8,128)(2,1)} %collective-permute-done.51.refs_3_, ...), custom_call_target="tpu_custom_call" | custom-call | bytes 25956352 | tf_op jit(solution)/shard_map/place_grads/pallas_call | solution.py:182
  976.9 63.4 %collective-permute-done.43 = f32[8192]{0:T(1024)S(1)} collective-permute-done((f32[8192]{0:T(1024)S(1)}, f32[8192]{0:T(1024)S(1)}, u32[]{:S(2)}, u32[]{:S(2)}) %collective-permute-start.43) | collective-permute-done | bytes 32800 | tf_op jit(solution)/shard_map/ppermute | solution.py:94
  1082.1 19.5 %collective-permute-done.56 = bf16[128,4224]{1,0:T(8,128)(2,1)S(1)} collective-permute-done((bf16[128,4224]{1,0:T(8,128)(2,1)S(1)}, bf16[128,4224]{1,0:T(8,128)(2,1)S(1)}, u32[]{:S(2)}, u32[]{:S(2)}) %collective-permute-start.56) | collective-permute-done | bytes 1081376 | tf_op jit(solution)/shard_map/ppermute | solution.py:94
  1131.2 38.2 %collective-permute-done.66 = bf16[256,512]{1,0:T(8,128)(2,1)S(1)} collective-permute-done((bf16[256,512]{1,0:T(8,128)(2,1)}, bf16[256,512]{1,0:T(8,128)(2,1)S(1)}, u32[]{:S(2)}, u32[]{:S(2)}) %collective-permute-start.66) | collective-permute-done | bytes 262176 | tf_op jit(solution)/shard_map/ppermute | solution.py:94
  1198.8 21.5 %collective-permute-done.48 = bf16[128,1536]{1,0:T(8,128)(2,1)S(1)} collective-permute-done((bf16[128,1536]{1,0:T(8,128)(2,1)S(1)}, bf16[128,1536]{1,0:T(8,128)(2,1)S(1)}, u32[]{:S(2)}, u32[]{:S(2)}) %collective-permute-start.48) | collective-permute-done | bytes 393248 | tf_op jit(solution)/shard_map/ppermute | solution.py:94
  (483 shorter events, 545.7 us)
Async XLA Ops:
  9.1 103.8 %all-gather.8.cloned.1.call-start = ((), (), s32[]{:S(2)}) async-start(), calls=%async_computation.6 | async-start | bytes 7667712 | tf_op jit(solution)/shard_map/all_gather | solution.py:700
  42.1 309.6 %all-gather.14.cloned.1.call-start = ((), (), s32[]{:S(2)}) async-start(), calls=%async_computation.9 | async-start | bytes 19464192 | tf_op jit(solution)/shard_map/all_gather | solution.py:700
  112.9 335.9 %all-gather.12.cloned.1.call-start = ((), (), s32[]{:S(2)}) async-start(), calls=%async_computation.8 | async-start | bytes 19464192 | tf_op jit(solution)/shard_map/all_gather | solution.py:700
  179.0 400.5 %all-gather.10.cloned.1.call-start = ((), (), s32[]{:S(2)}) async-start(), calls=%async_computation.7 | async-start | bytes 19464192 | tf_op jit(solution)/shard_map/all_gather | solution.py:700
  267.5 588.4 %reduce-scatter.12.cloned.1.call-start = ((), (), s32[]{:S(2)}) async-start(), calls=%async_computation.13 | async-start | bytes 10813440 | tf_op jit(solution)/shard_map/reduce_scatter | solution.py:735
  440.2 528.5 %reduce-scatter.10.cloned.1.call-start = ((), (), s32[]{:S(2)}) async-start(), calls=%async_computation.12 | async-start | bytes 10813440 | tf_op jit(solution)/shard_map/reduce_scatter | solution.py:735
  539.6 578.5 %reduce-scatter.8.cloned.1.call-start = ((), (), s32[]{:S(2)}) async-start(), calls=%async_computation.11 | async-start | bytes 10813440 | tf_op jit(solution)/shard_map/reduce_scatter | solution.py:735
  677.6 449.6 %reduce-scatter.14.cloned.1.call-start = ((), (), s32[]{:S(2)}) async-start(), calls=%async_computation.14 | async-start | bytes 2359296 | tf_op jit(solution)/shard_map/reduce_scatter | solution.py:703
  801.9 56.3 %collective-permute-start.70 = (f32[20480]{0:T(1024)S(1)}, f32[20480]{0:T(1024)S(1)}, u32[]{:S(2)}, u32[]{:S(2)}) collective-permute-start(f32[20480]{0:T(1024)S(1)} %pad_maximum_fusion.21), channel_id=1, source_target_pairs={{0,1},{1,0},{2,3},{3,2},{4,5},{5,4},{6,7},{7,6},{8,9},{9,8},{10,11... | collective-permute-start | bytes 245768 | tf_op jit(solution)/shard_map/ppermute | solution.py:156
  843.4 328.6 %reduce-scatter.6.cloned.1.call-start = ((), (), s32[]{:S(2)}) async-start(), calls=%async_computation.10 | async-start | bytes 3932160 | tf_op jit(solution)/shard_map/reduce_scatter | solution.py:735
  856.0 54.7 %collective-permute-start.50 = (bf16[256,4224]{1,0:T(8,128)(2,1)}, bf16[256,4224]{1,0:T(8,128)(2,1)}, u32[]{:S(2)}, u32[]{:S(2)}) collective-permute-start(bf16[256,4224]{1,0:T(8,128)(2,1)} %after.15.refs_1_), channel_id=1, source_target_pairs={{0,8},{8,0},{16,24},{24,16},{1,9},{9,1},{17,25},{25,17},{2,10},{10... | collective-permute-start | bytes 6488072 | tf_op jit(solution)/shard_map/ppermute | solution.py:94
  857.4 56.4 %collective-permute-start.51 = (bf16[256,4224]{1,0:T(8,128)(2,1)}, bf16[256,4224]{1,0:T(8,128)(2,1)}, u32[]{:S(2)}, u32[]{:S(2)}) collective-permute-start(bf16[256,4224]{1,0:T(8,128)(2,1)} %after.15.refs_1_), channel_id=1, source_target_pairs={{0,16},{8,24},{16,0},{24,8},{1,17},{9,25},{17,1},{25,9},{2,18},{10... | collective-permute-start | bytes 6488072 | tf_op jit(solution)/shard_map/ppermute | solution.py:94
  858.1 67.3 %collective-permute-start.45 = (bf16[1024,1536]{1,0:T(8,128)(2,1)}, bf16[1024,1536]{1,0:T(8,128)(2,1)}, u32[]{:S(2)}, u32[]{:S(2)}) collective-permute-start(bf16[1024,1536]{1,0:T(8,128)(2,1)} %grad_matmul.15.refs_2_), channel_id=1, source_target_pairs={{0,1},{1,0},{2,3},{3,2},{4,5},{5,4},{6,7},{7,6},{8,9},{9,8},{10,11... | collective-permute-start | bytes 9437192 | tf_op jit(solution)/shard_map/ppermute | solution.py:156
  903.7 70.9 %collective-permute-start.74 = (f32[20480]{0:T(1024)S(1)}, f32[20480]{0:T(1024)S(1)}, u32[]{:S(2)}, u32[]{:S(2)}) collective-permute-start(f32[20480]{0:T(1024)S(1)} %add.311), channel_id=1, source_target_pairs={{0,16},{8,24},{16,0},{24,8},{1,17},{9,25},{17,1},{25,9},{2,18},{10... | collective-permute-start | bytes 245768 | tf_op jit(solution)/shard_map/ppermute | solution.py:94
  925.4 117.1 %collective-permute-start.38 = (bf16[256,2048]{1,0:T(8,128)(2,1)}, bf16[256,2048]{1,0:T(8,128)(2,1)}, u32[]{:S(2)}, u32[]{:S(2)}) collective-permute-start(bf16[256,2048]{1,0:T(8,128)(2,1)} %pad_maximum_fusion.15), channel_id=1, source_target_pairs={{0,16},{8,24},{16,0},{24,8},{1,17},{9,25},{17,1},{25,9},{2,18},{10... | collective-permute-start | bytes 3145736 | tf_op jit(solution)/shard_map/ppermute | solution.py:94
  968.7 78.2 %collective-permute-start.54 = (bf16[256,4224]{1,0:T(8,128)(2,1)}, bf16[256,4224]{1,0:T(8,128)(2,1)}, u32[]{:S(2)}, u32[]{:S(2)}) collective-permute-start(bf16[256,4224]{1,0:T(8,128)(2,1)} %after.16.refs_1_), channel_id=1, source_target_pairs={{0,8},{8,0},{16,24},{24,16},{1,9},{9,1},{17,25},{25,17},{2,10},{10... | collective-permute-start | bytes 6488072 | tf_op jit(solution)/shard_map/ppermute | solution.py:94
  970.2 78.9 %collective-permute-start.55 = (bf16[256,4224]{1,0:T(8,128)(2,1)}, bf16[256,4224]{1,0:T(8,128)(2,1)}, u32[]{:S(2)}, u32[]{:S(2)}) collective-permute-start(bf16[256,4224]{1,0:T(8,128)(2,1)} %after.16.refs_1_), channel_id=1, source_target_pairs={{0,16},{8,24},{16,0},{24,8},{1,17},{9,25},{17,1},{25,9},{2,18},{10... | collective-permute-start | bytes 6488072 | tf_op jit(solution)/shard_map/ppermute | solution.py:94
  972.0 71.7 %collective-permute-start.36 = (bf16[256,2048]{1,0:T(8,128)(2,1)}, bf16[256,2048]{1,0:T(8,128)(2,1)}, u32[]{:S(2)}, u32[]{:S(2)}) collective-permute-start(bf16[256,2048]{1,0:T(8,128)(2,1)} %pad_maximum_fusion.14), channel_id=1, source_target_pairs={{0,8},{8,0},{16,24},{24,16},{1,9},{9,1},{17,25},{25,17},{2,10},{10... | collective-permute-start | bytes 3145736 | tf_op jit(solution)/shard_map/ppermute | solution.py:94
  974.7 65.6 %collective-permute-start.43 = (f32[8192]{0:T(1024)S(1)}, f32[8192]{0:T(1024)S(1)}, u32[]{:S(2)}, u32[]{:S(2)}) collective-permute-start(f32[8192]{0:T(1024)S(1)} %add.298), channel_id=1, source_target_pairs={{0,8},{8,0},{16,24},{24,16},{1,9},{9,1},{17,25},{25,17},{2,10},{10... | collective-permute-start | bytes 98312 | tf_op jit(solution)/shard_map/ppermute | solution.py:94
  1049.1 52.5 %collective-permute-start.56 = (bf16[128,4224]{1,0:T(8,128)(2,1)S(1)}, bf16[128,4224]{1,0:T(8,128)(2,1)S(1)}, u32[]{:S(2)}, u32[]{:S(2)}) collective-permute-start(bf16[128,4224]{1,0:T(8,128)(2,1)S(1)} %slice.469), channel_id=1, source_target_pairs={{0,16},{8,24},{16,0},{24,8},{1,17},{9,25},{17,1},{25,9},{2,18},{10... | collective-permute-start | bytes 3244040 | tf_op jit(solution)/shard_map/ppermute | solution.py:94
  1075.4 52.8 %collective-permute-start.33 = (bf16[128,2048]{1,0:T(8,128)(2,1)}, bf16[128,2048]{1,0:T(8,128)(2,1)}, u32[]{:S(2)}, u32[]{:S(2)}) collective-permute-start(bf16[128,2048]{1,0:T(8,128)(2,1)} %get-tuple-element.95), channel_id=1, source_target_pairs={{0,16},{8,24},{16,0},{24,8},{1,17},{9,25},{17,1},{25,9},{2,18},{10... | collective-permute-start | bytes 1572872 | tf_op jit(solution)/shard_map/ppermute | solution.py:94
  1078.5 93.5 %collective-permute-start.35 = (bf16[128,2048]{1,0:T(8,128)(2,1)}, bf16[128,2048]{1,0:T(8,128)(2,1)S(1)}, u32[]{:S(2)}, u32[]{:S(2)}) collective-permute-start(bf16[128,2048]{1,0:T(8,128)(2,1)} %get-tuple-element.96), channel_id=1, source_target_pairs={{0,8},{8,0},{16,24},{24,16},{1,9},{9,1},{17,25},{25,17},{2,10},{10... | collective-permute-start | bytes 1572872 | tf_op jit(solution)/shard_map/ppermute | solution.py:94
  1118.1 57.1 %collective-permute-start.58 = (bf16[256,4224]{1,0:T(8,128)(2,1)}, bf16[256,4224]{1,0:T(8,128)(2,1)}, u32[]{:S(2)}, u32[]{:S(2)}) collective-permute-start(bf16[256,4224]{1,0:T(8,128)(2,1)} %after.17.refs_1_), channel_id=1, source_target_pairs={{0,8},{8,0},{16,24},{24,16},{1,9},{9,1},{17,25},{25,17},{2,10},{10... | collective-permute-start | bytes 6488072 | tf_op jit(solution)/shard_map/ppermute | solution.py:94
  1119.7 57.4 %collective-permute-start.59 = (bf16[256,4224]{1,0:T(8,128)(2,1)}, bf16[256,4224]{1,0:T(8,128)(2,1)}, u32[]{:S(2)}, u32[]{:S(2)}) collective-permute-start(bf16[256,4224]{1,0:T(8,128)(2,1)} %after.17.refs_1_), channel_id=1, source_target_pairs={{0,16},{8,24},{16,0},{24,8},{1,17},{9,25},{17,1},{25,9},{2,18},{10... | collective-permute-start | bytes 6488072 | tf_op jit(solution)/shard_map/ppermute | solution.py:94
  (116 other events, 2366.0 us)
Sparse Core Ops, SparseCore 0:
  10.2 31.7 all-gather.5
  44.3 68.5 all-gather.7
  115.1 154.0 all-gather.13
  270.6 153.6 all-gather.11
  425.8 153.6 all-gather.9
  582.3 146.8 reduce-scatter.11
  732.1 152.8 reduce-scatter.9
  887.4 150.7 reduce-scatter.7
  1041.0 36.4 reduce-scatter.13
  1080.3 59.0 reduce-scatter.5

commit v2 on v1

--- a/solution.py
+++ b/solution.py
@@ -878,7 +878,6 @@
             waits = [shared_totals[2]]
         else:
             totals = place_grads(spread, own, experts_own, totals, waits)
-            waits = [totals[2]]
     wide_all = wide(tokens_all)
     d_gain_one = jnp.sum(wide(d_normed_part) * (wide_all * rms_scale(wide_all)), axis=0)
     d_tokens = d_resid + rms_back(d_normed, unit_one, scale_one, gain_one)
@@ -899,7 +898,7 @@
         block_out,
         d_tokens,
         own_part(late_grads[3 * D :]),
-        place_cols(peer_gather(grad_w_in), 3, [totals[1]]),
+        place_cols(peer_gather(after(grad_w_in, [late_grads, early_grads])), 3, [totals[1]]),
         own_part(late_grads[: 3 * D]),
         wide(jnp.concatenate(by_rank(peer_gather(grad_w_out)), axis=1)),
         own_part(early_grads[(EXPERTS + 1) * D :]),

time: 1270 us -> 1260 us (level)
    ppermute x65, waiting for transfers between devices: 407 us -> 372 us  [to_peer(): lax.ppermute(array, 'ctx', [(rank, rank ^ bits) for rank in range(size)])]
    reduce_scatter x4, waiting for transfers between devices: 0.03 us -> 30.5 us  [scatter_line(): lax.psum_scatter(grad, 'fsdp', scatter_dimension=0, axis_index_groups=lin...]
    unnamed x126 -> x132, local copies, waits for them, and re-layouts: 26 us -> 26.6 us
  transfers between devices with their start and end apart: 85 -> 85, of which waited for: 40 -> 41; matrix products, arithmetic and copies ran while one was open for 12% -> 12% of each run, Pallas kernels for 33% -> 33%
where the time goes in v2:
time: 1260 us; the launch traced here: 1250 us
  waiting for transfers between devices  561 us (45%)
  Pallas kernels  431 us (34%)
  other arithmetic  81.5 us (6%)
  local copies, waits for them, and re-layouts  78.5 us (6%)
  starting transfers between devices  73.8 us (6%)
  between operations  15.6 us (1%)
    pallas_call x25, Pallas kernels, own_call(): pl.pallas_call(body, out_shape=list(outs), grid_spec=pltpu.PrefetchScalar...  431 us
    ppermute x65, waiting for transfers between devices, to_peer(): lax.ppermute(array, 'ctx', [(rank, rank ^ bits) for rank in range(size)])  372 us
    all_gather x5, waiting for transfers between devices, gather_fsdp(): return lax.all_gather(array, 'fsdp', axis=0, tiled=True)  131 us
    ppermute x65, starting transfers between devices, to_peer(): lax.ppermute(array, 'ctx', [(rank, rank ^ bits) for rank in range(size)])  70.5 us
    reduce_scatter x4, waiting for transfers between devices, scatter_line(): lax.psum_scatter(grad, 'fsdp', scatter_dimension=0, axis_index_groups=lin...  30.5 us
    unnamed x132, local copies, waits for them, and re-layouts  26.6 us
    ppermute x10, waiting for transfers between devices, to_mate(): lax.ppermute(array, 'fsdp', [(rank, rank ^ bits) for rank in range(size)])  26.5 us
  transfers between devices with their start and end apart: 85, of which 41 were waited for; matrix products, arithmetic and copies ran while one was open for 12% of the time, Pallas kernels for 33%

profile of v2, /device:TPU:0, one launch (start us, length us, event | category | flops | bytes accessed | tf_op | source)
XLA Modules:
  0.0 1249.6 jit_solution(4787237417113920384)
XLA Ops:
  14.9 27.1 %all-gather.6.cloned.1.call-done.refs_1_.refs_5_ = bf16[2048,512]{1,0:T(8,128)(2,1)} async-done(((bf16[256,512]{1,0:T(8,128)(2,1)}), bf16[2048,512]{1,0:T(8,128)(2,1)}) %all-gather.6.cloned.1.call-update) | async-done | bytes 2097168 | tf_op jit(solution)/shard_map/all_gather | solution.py:700
  45.1 67.7 %all-gather.8.cloned.1.call-done.refs_2_.refs_1_ = bf16[2048,1664]{1,0:T(8,128)(2,1)} async-done(((bf16[256,1664]{1,0:T(8,128)(2,1)}), bf16[2048,1664]{1,0:T(8,128)(2,1)}) %all-gather.8.cloned.1.call-update) | async-done | bytes 6815760 | tf_op jit(solution)/shard_map/all_gather | solution.py:700
  163.0 16.0 %split_matmul.1 = (bf16[1024,2048]{1,0:T(8,128)(2,1)}, bf16[1024,1536]{1,0:T(8,128)(2,1)}) custom-call(bf16[1024,2048]{1,0:T(8,128)(2,1)} %constant_dynamic-update-slice_fusion.refs_0_, f32[1,2048]{1,0:T(1,128)} %bitcast.43, bf16[2048,1664]{1,0:T(8,128)(2,1)} %all-gather.8.cloned.1.call-done.refs_2_.refs_1_, f32[1,1536]{1,0:T(1,128)} %bitcast.51, ...), custom_call_target="tpu_custom_call" | custom-call | flops 6442450944 | bytes 19412992 | tf_op jit(solution)/shard_map/split_matmul/pallas_call | solution.py:182
  182.6 43.8 %collective-permute-done.4.refs_6_.refs_3_ = bf16[2048,512]{1,0:T(8,128)(2,1)S(1)} collective-permute-done((bf16[2048,512]{1,0:T(8,128)(2,1)S(1)}, bf16[2048,512]{1,0:T(8,128)(2,1)S(1)}, u32[]{:S(2)}, u32[]{:S(2)}) %collective-permute-start.4) | collective-permute-done | bytes 2097184 | tf_op jit(solution)/shard_map/ppermute | solution.py:94
  351.8 30.3 %unit_backward.3 = (bf16[1024,1408]{1,0:T(8,128)(2,1)}, bf16[1024,2816]{1,0:T(8,128)(2,1)}, f32[1024,1]{1,0:T(8,128)}) custom-call(bf16[1024,2048]{1,0:T(8,128)(2,1)} %copy-done.3, bf16[1024,2048]{1,0:T(8,128)(2,1)} %copy-done.6, bf16[2048,4224]{1,0:T(8,128)(2,1)} %all-gather.14.cloned.1.call-done.refs_2_.refs_1_.refs_3_, f32[1024,1]{1,0:T(8,128)} %add_divide_fusion.refs_3_), custom_call_target="tpu_custom_call" | custom-call | flops 17716740096 | bytes 34349056 | tf_op jit(solution)/shard_map/unit_backward/pallas_call | solution.py:182
  397.4 25.8 %back_matmul.6 = (f32[1024,2048]{1,0:T(8,128)}, f32[1024,2048]{1,0:T(8,128)}) custom-call(bf16[1024,2816]{1,0:T(8,128)(2,1)} %get-tuple-element.39.refs_2_.refs_0_, bf16[2048,4224]{1,0:T(8,128)(2,1)} %all-gather.14.cloned.1.call-done.refs_2_.refs_1_.refs_3_, bf16[1024,1408]{1,0:T(8,128)(2,1)} %get-tuple-element.40.refs_4_.refs_5_.refs_2_, ...), custom_call_target="tpu_custom_call" | custom-call | flops 17716740096 | bytes 60030976 | tf_op jit(solution)/shard_map/back_matmul/pallas_call | solution.py:182
  423.2 16.8 %grad_matmul.10.refs_4_ = bf16[1024,4224]{1,0:T(8,128)(2,1)} custom-call(s32[1]{0:T(128)} %bitcast.11.refs_0_, bf16[1024,2048]{1,0:T(8,128)(2,1)} %copy-done.3, bf16[1024,2816]{1,0:T(8,128)(2,1)} %get-tuple-element.39.refs_2_.refs_0_, bf16[1024,2048]{1,0:T(8,128)(2,1)} %copy-done.6, bf16[1024,1408]{1,0:T(8,128)(2,1)} %get-tuple-element.40.refs_4_.refs_5_.refs_2_, ...), custom_call_target="tpu_custom_call" | custom-call | flops 8858370048 | bytes 34340864 | tf_op jit(solution)/shard_map/grad_matmul/pallas_call | solution.py:182
  448.7 30.3 %unit_backward.4 = (bf16[1024,1408]{1,0:T(8,128)(2,1)}, bf16[1024,2816]{1,0:T(8,128)(2,1)}, f32[1024,1]{1,0:T(8,128)}) custom-call(bf16[1024,2048]{1,0:T(8,128)(2,1)} %copy-done.3, bf16[1024,2048]{1,0:T(8,128)(2,1)} %copy-done.6, bf16[2048,4224]{1,0:T(8,128)(2,1)} %all-gather.12.cloned.1.call-done.refs_2_.refs_1_.refs_4_, f32[1024,1]{1,0:T(8,128)} %copy.92.refs_3_, ...), custom_call_target="tpu_custom_call" | custom-call | flops 17716740096 | bytes 34349056 | tf_op jit(solution)/shard_map/unit_backward/pallas_call | solution.py:182
  498.5 28.5 %back_matmul.7 = (f32[1024,2048]{1,0:T(8,128)}, f32[1024,2048]{1,0:T(8,128)}) custom-call(bf16[1024,2816]{1,0:T(8,128)(2,1)} %get-tuple-element.42.refs_2_.refs_0_, bf16[2048,4224]{1,0:T(8,128)(2,1)} %all-gather.12.cloned.1.call-done.refs_2_.refs_1_.refs_4_, f32[1024,2048]{1,0:T(8,128)} %get-tuple-element.41.refs_6_.refs_2_, ...), custom_call_target="tpu_custom_call" | custom-call | flops 17716740096 | bytes 76808192 | tf_op jit(solution)/shard_map/back_matmul/pallas_call | solution.py:182
  527.1 16.4 %grad_matmul.12.refs_4_ = bf16[1024,4224]{1,0:T(8,128)(2,1)} custom-call(s32[1]{0:T(128)} %bitcast.11.refs_0_, bf16[1024,2048]{1,0:T(8,128)(2,1)} %copy-done.3, bf16[1024,2816]{1,0:T(8,128)(2,1)} %get-tuple-element.42.refs_2_.refs_0_, bf16[1024,2048]{1,0:T(8,128)(2,1)} %copy-done.6, bf16[1024,1408]{1,0:T(8,128)(2,1)} %get-tuple-element.43.refs_4_.refs_5_.refs_3_, ...), custom_call_target="tpu_custom_call" | custom-call | flops 8858370048 | bytes 34340864 | tf_op jit(solution)/shard_map/grad_matmul/pallas_call | solution.py:182
  543.5 36.0 %all-gather.10.cloned.1.call-done.refs_2_.refs_1_ = bf16[2048,4224]{1,0:T(8,128)(2,1)} async-done(((bf16[256,4224]{1,0:T(8,128)(2,1)}), bf16[2048,4224]{1,0:T(8,128)(2,1)}) %all-gather.10.cloned.1.call-update) | async-done | bytes 17301520 | tf_op jit(solution)/shard_map/all_gather | solution.py:700
  579.5 30.9 %unit_backward.5 = (bf16[1024,1408]{1,0:T(8,128)(2,1)}, bf16[1024,2816]{1,0:T(8,128)(2,1)}, f32[1024,1]{1,0:T(8,128)}) custom-call(bf16[1024,2048]{1,0:T(8,128)(2,1)} %copy-done.3, bf16[1024,2048]{1,0:T(8,128)(2,1)} %copy-done.6, bf16[2048,4224]{1,0:T(8,128)(2,1)} %all-gather.10.cloned.1.call-done.refs_2_.refs_1_, f32[1024,1]{1,0:T(8,128)} %copy.93.refs_3_, ...), custom_call_target="tpu_custom_call" | custom-call | flops 17716740096 | bytes 34349056 | tf_op jit(solution)/shard_map/unit_backward/pallas_call | solution.py:182
  612.8 19.2 %back_matmul.8.refs_5_ = bf16[1024,2048]{1,0:T(8,128)(2,1)} custom-call(bf16[1024,2816]{1,0:T(8,128)(2,1)} %get-tuple-element.48.refs_0_.refs_2_, bf16[2048,4224]{1,0:T(8,128)(2,1)} %all-gather.10.cloned.1.call-done.refs_2_.refs_1_, bf16[1024,18]{1,0:T(8,128)(2,1)} %copy.96.refs_2_, bf16[2048,18]{1,0:T(8,128)(2,1)} %pad_maximum_fusion.20.refs_3_, ...), custom_call_target="tpu_custom_call" | custom-call | flops 11886657536 | bytes 35762176 | tf_op jit(solution)/shard_map/back_matmul/pallas_call | solution.py:182
  652.1 21.3 %collective-permute-done.26 = bf16[256,2048]{1,0:T(8,128)(2,1)S(1)} collective-permute-done((bf16[256,2048]{1,0:T(8,128)(2,1)S(1)}, bf16[256,2048]{1,0:T(8,128)(2,1)S(1)}, u32[]{:S(2)}, u32[]{:S(2)}) %collective-permute-start.26) | collective-permute-done | bytes 1048608 | tf_op jit(solution)/shard_map/ppermute | solution.py:94
  699.1 16.4 %grad_matmul.14.refs_8_ = bf16[1024,4224]{1,0:T(8,128)(2,1)} custom-call(s32[1]{0:T(128)} %bitcast.11.refs_0_, bf16[1024,2048]{1,0:T(8,128)(2,1)} %copy-done.3, bf16[1024,2816]{1,0:T(8,128)(2,1)} %get-tuple-element.48.refs_0_.refs_2_, bf16[1024,2048]{1,0:T(8,128)(2,1)} %copy-done.6, bf16[1024,1408]{1,0:T(8,128)(2,1)} %get-tuple-element.46.refs_5_.refs_4_.refs_0_, ...), custom_call_target="tpu_custom_call" | custom-call | flops 8858370048 | bytes 34340864 | tf_op jit(solution)/shard_map/grad_matmul/pallas_call | solution.py:182
  737.9 43.9 %collective-permute-done.69 = bf16[2048,512]{1,0:T(8,128)(2,1)S(1)} collective-permute-done((bf16[2048,512]{1,0:T(8,128)(2,1)S(1)}, bf16[2048,512]{1,0:T(8,128)(2,1)S(1)}, u32[]{:S(2)}, u32[]{:S(2)}) %collective-permute-start.69) | collective-permute-done | bytes 2097184 | tf_op jit(solution)/shard_map/ppermute | solution.py:94
  785.7 21.0 %collective-permute-done.68 = bf16[1024,512]{1,0:T(8,128)(2,1)S(1)} collective-permute-done((bf16[1024,512]{1,0:T(8,128)(2,1)S(1)}, bf16[1024,512]{1,0:T(8,128)(2,1)S(1)}, u32[]{:S(2)}, u32[]{:S(2)}) %collective-permute-start.68) | collective-permute-done | bytes 1048608 | tf_op jit(solution)/shard_map/ppermute | solution.py:94
  826.4 21.1 %attend_back.1.refs_1_.refs_2_.refs_0_ = bf16[1024,1536]{1,0:T(8,128)(2,1)} custom-call(bf16[1024,1536]{1,0:T(8,128)(2,1)} %get-tuple-element.37.refs_0_.refs_1_.refs_2_, bf16[1024,1536]{1,0:T(8,128)(2,1)} %get-tuple-element.37.refs_0_.refs_1_.refs_2_, bf16[1024,1536]{1,0:T(8,128)(2,1)} %get-tuple-element.37.refs_0_.refs_1_.refs_2_, ...), custom_call_target="tpu_custom_call" | custom-call | flops 5368709120 | bytes 14704640 | tf_op jit(solution)/shard_map/attend_back/pallas_call | solution.py:182
  931.4 36.7 %collective-permute-done.43 = f32[8192]{0:T(1024)S(1)} collective-permute-done((f32[8192]{0:T(1024)S(1)}, f32[8192]{0:T(1024)S(1)}, u32[]{:S(2)}, u32[]{:S(2)}) %collective-permute-start.43) | collective-permute-done | bytes 32800 | tf_op jit(solution)/shard_map/ppermute | solution.py:94
  975.4 16.8 %collective-permute-done.44 = f32[8192]{0:T(1024)S(1)} collective-permute-done((f32[8192]{0:T(1024)S(1)}, f32[8192]{0:T(1024)S(1)}, u32[]{:S(2)}, u32[]{:S(2)}) %collective-permute-start.44) | collective-permute-done | bytes 32800 | tf_op jit(solution)/shard_map/ppermute | solution.py:94
  1021.9 23.2 %place_grads.3 = (f32[256,11264]{1,0:T(8,128)}, f32[256,5632]{1,0:T(8,128)}, f32[8,128]{1,0:T(8,128)}) custom-call(s32[1]{0:T(128)} %bitcast.17.refs_0_, bf16[256,4224]{1,0:T(8,128)(2,1)} %after.17.refs_1_, bf16[256,4224]{1,0:T(8,128)(2,1)} %collective-permute-done.55.refs_2_, bf16[256,4224]{1,0:T(8,128)(2,1)} %collective-permute-done.56.refs_3_, ...), custom_call_target="tpu_custom_call" | custom-call | bytes 25956352 | tf_op jit(solution)/shard_map/place_grads/pallas_call | solution.py:182
  1052.3 41.1 %collective-permute-done.71 = bf16[256,512]{1,0:T(8,128)(2,1)S(1)} collective-permute-done((bf16[256,512]{1,0:T(8,128)(2,1)}, bf16[256,512]{1,0:T(8,128)(2,1)S(1)}, u32[]{:S(2)}, u32[]{:S(2)}) %collective-permute-start.71) | collective-permute-done | bytes 262176 | tf_op jit(solution)/shard_map/ppermute | solution.py:94
  1107.5 30.5 %reduce-scatter.6.cloned.1.call-done.refs_0_ = bf16[256,1536]{1,0:T(8,128)(2,1)} async-done(((bf16[1024,1536]{1,0:T(8,128)(2,1)}), bf16[256,1536]{1,0:T(8,128)(2,1)}) %reduce-scatter.6.cloned.1.call-update) | async-done | bytes 786448 | tf_op jit(solution)/shard_map/reduce_scatter | solution.py:735
  1171.4 23.9 %collective-permute-done.53 = bf16[128,1536]{1,0:T(8,128)(2,1)S(1)} collective-permute-done((bf16[128,1536]{1,0:T(8,128)(2,1)S(1)}, bf16[128,1536]{1,0:T(8,128)(2,1)S(1)}, u32[]{:S(2)}, u32[]{:S(2)}) %collective-permute-start.53) | collective-permute-done | bytes 393248 | tf_op jit(solution)/shard_map/ppermute | solution.py:94
  (491 shorter events, 549.2 us)
Async XLA Ops:
  9.1 103.8 %all-gather.8.cloned.1.call-start = ((), (), s32[]{:S(2)}) async-start(), calls=%async_computation.6 | async-start | bytes 7667712 | tf_op jit(solution)/shard_map/all_gather | solution.py:700
  42.1 309.8 %all-gather.14.cloned.1.call-start = ((), (), s32[]{:S(2)}) async-start(), calls=%async_computation.9 | async-start | bytes 19464192 | tf_op jit(solution)/shard_map/all_gather | solution.py:700
  112.9 335.8 %all-gather.12.cloned.1.call-start = ((), (), s32[]{:S(2)}) async-start(), calls=%async_computation.8 | async-start | bytes 19464192 | tf_op jit(solution)/shard_map/all_gather | solution.py:700
  179.0 400.4 %all-gather.10.cloned.1.call-start = ((), (), s32[]{:S(2)}) async-start(), calls=%async_computation.7 | async-start | bytes 19464192 | tf_op jit(solution)/shard_map/all_gather | solution.py:700
  267.5 630.0 %reduce-scatter.10.cloned.1.call-start = ((), (), s32[]{:S(2)}) async-start(), calls=%async_computation.12 | async-start | bytes 10813440 | tf_op jit(solution)/shard_map/reduce_scatter | solution.py:735
  440.0 605.1 %reduce-scatter.12.cloned.1.call-start = ((), (), s32[]{:S(2)}) async-start(), calls=%async_computation.13 | async-start | bytes 10813440 | tf_op jit(solution)/shard_map/reduce_scatter | solution.py:735
  612.7 437.6 %reduce-scatter.14.cloned.1.call-start = ((), (), s32[]{:S(2)}) async-start(), calls=%async_computation.14 | async-start | bytes 2359296 | tf_op jit(solution)/shard_map/reduce_scatter | solution.py:703
  647.5 51.6 %collective-permute-start.28 = (bf16[1024,4224]{1,0:T(8,128)(2,1)}, bf16[1024,4224]{1,0:T(8,128)(2,1)}, u32[]{:S(2)}, u32[]{:S(2)}) collective-permute-start(bf16[1024,4224]{1,0:T(8,128)(2,1)} %grad_matmul.13.refs_3_), channel_id=1, source_target_pairs={{0,1},{1,0},{2,3},{3,2},{4,5},{5,4},{6,7},{7,6},{8,9},{9,8},{10,11... | collective-permute-start | bytes 25952264 | tf_op jit(solution)/shard_map/ppermute | solution.py:156
  735.6 46.2 %collective-permute-start.69 = (bf16[2048,512]{1,0:T(8,128)(2,1)S(1)}, bf16[2048,512]{1,0:T(8,128)(2,1)S(1)}, u32[]{:S(2)}, u32[]{:S(2)}) collective-permute-start(bf16[2048,512]{1,0:T(8,128)(2,1)S(1)} %pad_maximum_fusion.7), channel_id=1, source_target_pairs={{0,16},{8,24},{16,0},{24,8},{1,17},{9,25},{17,1},{25,9},{2,18},{10... | collective-permute-start | bytes 6291464 | tf_op jit(solution)/shard_map/ppermute | solution.py:94
  809.5 286.8 %reduce-scatter.8.cloned.1.call-start = ((), (), s32[]{:S(2)}) async-start(), calls=%async_computation.11 | async-start | bytes 10813440 | tf_op jit(solution)/shard_map/reduce_scatter | solution.py:735
  810.2 327.8 %reduce-scatter.6.cloned.1.call-start = ((), (), s32[]{:S(2)}) async-start(), calls=%async_computation.10 | async-start | bytes 3932160 | tf_op jit(solution)/shard_map/reduce_scatter | solution.py:735
  854.9 52.3 %collective-permute-start.45 = (bf16[1024,1536]{1,0:T(8,128)(2,1)}, bf16[1024,1536]{1,0:T(8,128)(2,1)}, u32[]{:S(2)}, u32[]{:S(2)}) collective-permute-start(bf16[1024,1536]{1,0:T(8,128)(2,1)} %grad_matmul.15.refs_2_), channel_id=1, source_target_pairs={{0,1},{1,0},{2,3},{3,2},{4,5},{5,4},{6,7},{7,6},{8,9},{9,8},{10,11... | collective-permute-start | bytes 9437192 | tf_op jit(solution)/shard_map/ppermute | solution.py:156
  897.6 72.1 %collective-permute-start.55 = (bf16[256,4224]{1,0:T(8,128)(2,1)}, bf16[256,4224]{1,0:T(8,128)(2,1)}, u32[]{:S(2)}, u32[]{:S(2)}) collective-permute-start(bf16[256,4224]{1,0:T(8,128)(2,1)} %after.17.refs_1_), channel_id=1, source_target_pairs={{0,8},{8,0},{16,24},{24,16},{1,9},{9,1},{17,25},{25,17},{2,10},{10... | collective-permute-start | bytes 6488072 | tf_op jit(solution)/shard_map/ppermute | solution.py:94
  898.7 72.3 %collective-permute-start.56 = (bf16[256,4224]{1,0:T(8,128)(2,1)}, bf16[256,4224]{1,0:T(8,128)(2,1)}, u32[]{:S(2)}, u32[]{:S(2)}) collective-permute-start(bf16[256,4224]{1,0:T(8,128)(2,1)} %after.17.refs_1_), channel_id=1, source_target_pairs={{0,16},{8,24},{16,0},{24,8},{1,17},{9,25},{17,1},{25,9},{2,18},{10... | collective-permute-start | bytes 6488072 | tf_op jit(solution)/shard_map/ppermute | solution.py:94
  918.3 74.4 %collective-permute-start.38 = (bf16[256,2048]{1,0:T(8,128)(2,1)}, bf16[256,2048]{1,0:T(8,128)(2,1)}, u32[]{:S(2)}, u32[]{:S(2)}) collective-permute-start(bf16[256,2048]{1,0:T(8,128)(2,1)} %pad_maximum_fusion.15), channel_id=1, source_target_pairs={{0,16},{8,24},{16,0},{24,8},{1,17},{9,25},{17,1},{25,9},{2,18},{10... | collective-permute-start | bytes 3145736 | tf_op jit(solution)/shard_map/ppermute | solution.py:94
  926.6 70.5 %collective-permute-start.36 = (bf16[256,2048]{1,0:T(8,128)(2,1)}, bf16[256,2048]{1,0:T(8,128)(2,1)}, u32[]{:S(2)}, u32[]{:S(2)}) collective-permute-start(bf16[256,2048]{1,0:T(8,128)(2,1)} %pad_maximum_fusion.14), channel_id=1, source_target_pairs={{0,8},{8,0},{16,24},{24,16},{1,9},{9,1},{17,25},{25,17},{2,10},{10... | collective-permute-start | bytes 3145736 | tf_op jit(solution)/shard_map/ppermute | solution.py:94
  1001.7 47.8 %collective-permute-start.39 = (bf16[128,2048]{1,0:T(8,128)(2,1)}, bf16[128,2048]{1,0:T(8,128)(2,1)S(1)}, u32[]{:S(2)}, u32[]{:S(2)}) collective-permute-start(bf16[128,2048]{1,0:T(8,128)(2,1)} %get-tuple-element.88), channel_id=1, source_target_pairs={{0,8},{8,0},{16,24},{24,16},{1,9},{9,1},{17,25},{25,17},{2,10},{10... | collective-permute-start | bytes 1572872 | tf_op jit(solution)/shard_map/ppermute | solution.py:94
  1005.2 91.1 %collective-permute-start.33 = (bf16[128,2048]{1,0:T(8,128)(2,1)}, bf16[128,2048]{1,0:T(8,128)(2,1)}, u32[]{:S(2)}, u32[]{:S(2)}) collective-permute-start(bf16[128,2048]{1,0:T(8,128)(2,1)} %get-tuple-element.93), channel_id=1, source_target_pairs={{0,16},{8,24},{16,0},{24,8},{1,17},{9,25},{17,1},{25,9},{2,18},{10... | collective-permute-start | bytes 1572872 | tf_op jit(solution)/shard_map/ppermute | solution.py:94
  1019.0 79.3 %collective-permute-start.35 = (bf16[128,2048]{1,0:T(8,128)(2,1)}, bf16[128,2048]{1,0:T(8,128)(2,1)S(1)}, u32[]{:S(2)}, u32[]{:S(2)}) collective-permute-start(bf16[128,2048]{1,0:T(8,128)(2,1)} %get-tuple-element.94), channel_id=1, source_target_pairs={{0,8},{8,0},{16,24},{24,16},{1,9},{9,1},{17,25},{25,17},{2,10},{10... | collective-permute-start | bytes 1572872 | tf_op jit(solution)/shard_map/ppermute | solution.py:94
  1045.2 95.7 %collective-permute-start.63 = (bf16[256,4224]{1,0:T(8,128)(2,1)}, bf16[256,4224]{1,0:T(8,128)(2,1)}, u32[]{:S(2)}, u32[]{:S(2)}) collective-permute-start(bf16[256,4224]{1,0:T(8,128)(2,1)} %after.19.refs_1_), channel_id=1, source_target_pairs={{0,8},{8,0},{16,24},{24,16},{1,9},{9,1},{17,25},{25,17},{2,10},{10... | collective-permute-start | bytes 6488072 | tf_op jit(solution)/shard_map/ppermute | solution.py:94
  1045.8 95.6 %collective-permute-start.64 = (bf16[256,4224]{1,0:T(8,128)(2,1)}, bf16[256,4224]{1,0:T(8,128)(2,1)}, u32[]{:S(2)}, u32[]{:S(2)}) collective-permute-start(bf16[256,4224]{1,0:T(8,128)(2,1)} %after.19.refs_1_), channel_id=1, source_target_pairs={{0,16},{8,24},{16,0},{24,8},{1,17},{9,25},{17,1},{25,9},{2,18},{10... | collective-permute-start | bytes 6488072 | tf_op jit(solution)/shard_map/ppermute | solution.py:94
  1098.3 68.2 %collective-permute-start.59 = (bf16[256,4224]{1,0:T(8,128)(2,1)}, bf16[256,4224]{1,0:T(8,128)(2,1)}, u32[]{:S(2)}, u32[]{:S(2)}) collective-permute-start(bf16[256,4224]{1,0:T(8,128)(2,1)} %after.18.refs_1_), channel_id=1, source_target_pairs={{0,8},{8,0},{16,24},{24,16},{1,9},{9,1},{17,25},{25,17},{2,10},{10... | collective-permute-start | bytes 6488072 | tf_op jit(solution)/shard_map/ppermute | solution.py:94
  1102.6 65.9 %collective-permute-start.60 = (bf16[256,4224]{1,0:T(8,128)(2,1)}, bf16[256,4224]{1,0:T(8,128)(2,1)}, u32[]{:S(2)}, u32[]{:S(2)}) collective-permute-start(bf16[256,4224]{1,0:T(8,128)(2,1)} %after.18.refs_1_), channel_id=1, source_target_pairs={{0,16},{8,24},{16,0},{24,8},{1,17},{9,25},{17,1},{25,9},{2,18},{10... | collective-permute-start | bytes 6488072 | tf_op jit(solution)/shard_map/ppermute | solution.py:94
  1168.6 47.7 %collective-permute-start.61 = (bf16[128,4224]{1,0:T(8,128)(2,1)S(1)}, bf16[128,4224]{1,0:T(8,128)(2,1)S(1)}, u32[]{:S(2)}, u32[]{:S(2)}) collective-permute-start(bf16[128,4224]{1,0:T(8,128)(2,1)S(1)} %slice.469), channel_id=1, source_target_pairs={{0,16},{8,24},{16,0},{24,8},{1,17},{9,25},{17,1},{25,9},{2,18},{10... | collective-permute-start | bytes 3244040 | tf_op jit(solution)/shard_map/ppermute | solution.py:94
  (119 other events, 2295.0 us)
Sparse Core Ops, SparseCore 0:
  10.2 31.7 all-gather.5
  44.3 68.5 all-gather.7
  115.1 154.0 all-gather.13
  270.6 153.6 all-gather.11
  425.8 153.6 all-gather.9
  582.3 146.8 reduce-scatter.9
  732.1 152.8 reduce-scatter.11
  887.9 36.3 reduce-scatter.13
  926.6 147.4 reduce-scatter.7
  1076.9 61.0 reduce-scatter.5
